TPU v7x, 128 devices: a whole 4x4x4 slice. The times are simulated.
128 devices in a mesh: grp: 4 (over x_lo, core), ctx: 8 (over y, x_hi), tp: 4 (over z).
Axes of the slice: x: 4 (x_hi: 2, x_lo: 2; x = x_hi * 2 + x_lo), y: 4, z: 4, core: 2. Of those that a mesh axis runs over, the one named last changes fastest.
Arguments:
- enc_pre: bfloat16 [2048, 8192], P('ctx', ('grp', 'tp')), may hold values from -6 to 6
- proj_weight: bfloat16 [8192, 8192], P(('grp', 'tp')), may hold values from -0.09375 to 0.09375
- prompt_hidden: bfloat16 [6144, 8192], P('ctx', ('grp', 'tp')), may hold values from -800 to 800
- norm_gain: bfloat16 [8192], replicated, may hold values from 0.099609375 to 1.8984375
- q_weight: bfloat16 [8192, 8192], P(None, ('grp', 'tp')), may hold values from -24 to 24
- kv_weight: bfloat16 [8192, 2048], P(None, ('grp', 'tp')), may hold values from -1 to 1
- tile_starts: int32 [8], replicated, may hold values from 0 to 5888, as said below
- prompt_lengths: int32 [3], replicated, may hold values from 1 to 3840, 6144 in all
Outputs:
- attended: bfloat16 [6144, 8192], P('ctx', ('grp', 'tp'))
Inputs may be any that keep to these rules, and one draw needn't show every extreme that they name: The 256 visual rows of tile t go to positions tile_starts[t] to tile_starts[t] + 255, and no two tiles share a position.
All inputs are finite; a program needn't handle non-finite values.
Results may differ from a plain program's by a relative error of at most 0.0059.
Values may be sent and summed in bfloat16 or wider, within the bound.
No kernel may reach another device: no remote copies, remote signals or barrier semaphores. Data moves between devices by JAX's collectives and lax.ppermute only.
A program may use at most 128 MiB of HBM per device.

v0:
```python
import math

import jax
import jax.numpy as jnp
from jax import lax
from jax.sharding import PartitionSpec as P

HEAD_WIDTH = 128
VTOK = 256


ROPE_BASE = 1000000.0
NORM_EPSILON = 1e-06
MASKED_SCORE = -1e30


def partner_2(block, axis, stride):
    count = lax.axis_size(axis)
    route = []
    for low in range(count):
        high = low | 1 << stride
        if high != low and high < count:
            route += [(low, high), (high, low)]
    return lax.ppermute(block, axis, route)


def rotary(values, positions):
    half_dim = values.shape[-1] // 2
    frequency = ROPE_BASE ** (-2.0 * jnp.arange(half_dim, dtype=jnp.float32) / values.shape[-1])
    angles = positions.astype(jnp.float32)[:, None] * frequency[None, :]
    cosine = jnp.cos(angles)[:, None, :]
    sine_part = jnp.sin(angles)[:, None, :]
    front_half = values[..., :half_dim]
    back_half = values[..., half_dim:]
    return jnp.concatenate(
        [front_half * cosine - back_half * sine_part, back_half * cosine + front_half * sine_part],
        axis=-1,
    )


def doc_layout(prompt_lengths, positions):
    doc_ends = jnp.cumsum(prompt_lengths)
    document = jnp.sum((positions[:, None] >= doc_ends[None, :]).astype(jnp.int32), axis=1)
    doc_starts = doc_ends - prompt_lengths
    prompt_ids = jnp.arange(prompt_lengths.shape[0], dtype=jnp.int32)
    doc_begin = jnp.sum(
        jnp.where(document[:, None] == prompt_ids[None, :], doc_starts[None, :], 0), axis=1
    )
    return (document, positions - doc_begin)


def shards(
    enc_pre, proj_weight, prompt_hidden, norm_gain, q_weight, kv_weight, tile_starts, prompt_lengths
):
    tok_rows = prompt_hidden.shape[0]
    tile_count = tile_starts.shape[0]
    offset = lax.axis_index("ctx") * tok_rows
    rows_here = offset + jnp.arange(tok_rows, dtype=jnp.int32)
    span_rows = rows_here[:, None] - tile_starts[None, :]
    is_visual = jnp.any((span_rows >= 0) & (span_rows < VTOK), axis=1)
    activated = jax.nn.gelu(enc_pre.astype(jnp.float32), approximate=False).astype(jnp.bfloat16)
    my_share = lax.psum_scatter(
        lax.dot_general(
            proj_weight, activated, (((0,), (1,)), ((), ())), preferred_element_type=jnp.float32
        ),
        ("grp", "tp"),
        scatter_dimension=0,
        tiled=True,
    ).astype(jnp.bfloat16)
    piece = lax.all_gather(my_share, "ctx", axis=1, tiled=True)
    vis_index = jnp.arange(piece.shape[1], dtype=jnp.int32)
    tile_index = vis_index // VTOK
    picked = tile_index[:, None] == jnp.arange(tile_count, dtype=jnp.int32)[None, :]
    target = jnp.sum(jnp.where(picked, tile_starts[None, :], 0), axis=1) + vis_index % VTOK
    routed = lax.dot_general(
        (target[None, :] == rows_here[:, None]).astype(jnp.bfloat16),
        piece,
        (((1,), (1,)), ((), ())),
        preferred_element_type=jnp.float32,
    )
    assembled = jnp.where(is_visual[:, None], routed.astype(jnp.bfloat16), prompt_hidden)
    hidden = lax.all_gather(assembled, ("grp", "tp"), axis=1, tiled=True)
    hidden_f32 = hidden.astype(jnp.float32)
    inv_rms = lax.rsqrt(jnp.mean(hidden_f32 * hidden_f32, axis=1, keepdims=True) + NORM_EPSILON)
    normed = (hidden_f32 * inv_rms * norm_gain.astype(jnp.float32)[None, :]).astype(jnp.bfloat16)
    document, inner_pos = doc_layout(prompt_lengths, rows_here)
    heads_here = q_weight.shape[1] // HEAD_WIDTH
    queries = jnp.dot(normed, q_weight, preferred_element_type=jnp.float32).reshape(
        tok_rows, heads_here, HEAD_WIDTH
    )
    queries = (
        rotary(queries, inner_pos).astype(jnp.bfloat16).reshape(tok_rows * heads_here, HEAD_WIDTH)
    )
    own_half = jnp.dot(normed, kv_weight, preferred_element_type=jnp.float32).astype(jnp.bfloat16)
    partner = partner_2(own_half, "tp", 0)
    half_dim = HEAD_WIDTH // 2
    lower_first = lax.axis_index("tp") % 2 == 0
    lower_half = jnp.where(lower_first, own_half, partner)
    upper_half = jnp.where(lower_first, partner, own_half)
    projected_key_rows = jnp.concatenate(
        [lower_half[:, :half_dim], upper_half[:, :half_dim]], axis=1
    )
    projected_value_rows = jnp.concatenate(
        [lower_half[:, half_dim:], upper_half[:, half_dim:]], axis=1
    )
    projected_key_rows = rotary(projected_key_rows.astype(jnp.float32)[:, None, :], inner_pos)[
        :, 0, :
    ].astype(jnp.bfloat16)
    query_pos = jnp.repeat(rows_here, heads_here)
    query_doc = jnp.repeat(document, heads_here)
    last_row = offset + tok_rows - 1
    query_count = tok_rows * heads_here
    initial = (
        jnp.full((query_count,), MASKED_SCORE, jnp.float32),
        jnp.zeros((query_count,), jnp.float32),
        jnp.zeros((query_count, HEAD_WIDTH), jnp.float32),
    )
    key_block = lax.all_gather(projected_key_rows, "ctx", axis=0, tiled=True)
    value_block = lax.all_gather(projected_value_rows, "ctx", axis=0, tiled=True)
    block_count = key_block.shape[0] // tok_rows
    key_split = key_block.reshape(block_count, tok_rows, HEAD_WIDTH)
    value_split = value_block.reshape(block_count, tok_rows, HEAD_WIDTH)
    firsts = tok_rows * jnp.arange(block_count, dtype=jnp.int32)

    def key_step(state, item):
        keys_here, values_here, first_key = item

        def update(current):
            running_max, denom_sum, accumulated = current
            key_pos = first_key + jnp.arange(tok_rows, dtype=jnp.int32)
            key_doc = doc_layout(prompt_lengths, key_pos)[0]
            scores = lax.dot_general(
                queries, keys_here, (((1,), (1,)), ((), ())), preferred_element_type=jnp.float32
            ) / math.sqrt(HEAD_WIDTH)
            allowed = (key_pos[None, :] <= query_pos[:, None]) & (
                key_doc[None, :] == query_doc[:, None]
            )
            scores = jnp.where(allowed, scores, MASKED_SCORE)
            new_max = jnp.maximum(running_max, jnp.max(scores, axis=1))
            weights = jnp.where(allowed, jnp.exp(scores - new_max[:, None]), 0.0)
            rescale = jnp.exp(running_max - new_max)
            denom_sum = denom_sum * rescale + jnp.sum(weights, axis=1)
            accumulated = accumulated * rescale[:, None] + jnp.dot(
                weights.astype(jnp.bfloat16), values_here, preferred_element_type=jnp.float32
            )
            return (new_max, denom_sum, accumulated)

        return (lax.cond(first_key <= last_row, update, lambda current: current, state), None)

    result, ignored = lax.scan(key_step, initial, (key_split, value_split, firsts))
    running_max, denom_sum, accumulated = result
    attended = (accumulated / denom_sum[:, None]).astype(jnp.bfloat16)
    return attended.reshape(tok_rows, heads_here * HEAD_WIDTH)


def solution(mesh):
    in_specs = (
        P("ctx", ("grp", "tp")),
        P(("grp", "tp"), None),
        P("ctx", ("grp", "tp")),
        P(),
        P(None, ("grp", "tp")),
        P(None, ("grp", "tp")),
        P(),
        P(),
    )
    out_specs = P("ctx", ("grp", "tp"))
    return jax.shard_map(shards, mesh=mesh, in_specs=in_specs, out_specs=out_specs, check_vma=False)
```

profile of v0, /device:TPU:30, one launch (start us, length us, event | category | flops | bytes accessed | tf_op | source)
XLA Modules:
  0.0 514.1 jit_solution(6504584537779575157)
XLA Ops:
  6.5 10.2 %convolution_bitcast_fusion = f32[8192,256]{0,1:T(8,128)} fusion(bf16[512,8192]{1,0:T(8,128)(2,1)} %param.13, bf16[256,512]{1,0:T(8,128)(2,1)} %param.12), kind=kOutput, calls=%fused_computation.29 | convolution fusion | flops 2156134400 | bytes 17039360 | tf_op jit(solution)/shard_map/dot_general | solution.py:63
  16.8 97.7 %reduce-scatter.2.cloned.1.call-done = f32[512,256]{0,1:T(8,128)} async-done(((f32[8192,256]{0,1:T(8,128)}), f32[512,256]{0,1:T(8,128)}) %reduce-scatter.2.cloned.1.call-update) | async-done | bytes 524304 | tf_op jit(solution)/shard_map/reduce_scatter | solution.py:62
  114.5 1.8 convert_element_type.71
  116.6 54.0 %all-gather.6.cloned.1.call-done = bf16[512,2048]{0,1:T(8,128)(2,1)} async-done(((bf16[512,256]{0,1:T(8,128)(2,1)}), bf16[512,2048]{0,1:T(8,128)(2,1)}) %all-gather.6.cloned.1.call-update) | async-done | bytes 2097168 | tf_op jit(solution)/shard_map/all_gather | solution.py:70
  170.6 4.5 fusion.36
  175.2 75.6 %all-gather.8.cloned.1.call-done = bf16[768,8192]{1,0:T(8,128)(2,1)} async-done(((bf16[768,512]{1,0:T(8,128)(2,1)}), bf16[768,8192]{1,0:T(8,128)(2,1)}) %all-gather.8.cloned.1.call-update) | async-done | bytes 12582928 | tf_op jit(solution)/shard_map/all_gather | solution.py:82
  250.8 7.1 %fusion.22 = f32[768]{0:T(1024)S(1)} fusion(bf16[768,8192]{1,0:T(8,128)(2,1)} %all-gather.8.cloned.1.call-done), kind=kLoop, calls=%fused_computation.26 | loop fusion | flops 18873600 | bytes 12585984 | tf_op jit(solution)/shard_map/reduce_sum | solution.py:84
  257.9 9.0 %fusion.39 = bf16[768,128]{0,1:T(8,128)(2,1)S(1)} fusion(bf16[8192,128]{1,0:T(8,128)(2,1)S(1)} %copy-done, bf16[768,8192]{1,0:T(8,128)(2,1)} %all-gather.8.cloned.1.call-done, f32[8192]{0:T(1024)S(1)} %convert_element_type.74, f32[768]{0:T(1024)S(1)} %add_rsqrt_fusion), kind=kOutput, calls=%fused_computation.39 | convolution fusion | flops 1635876864 | bytes 14912512 | tf_op jit(solution)/shard_map/dot_general | solution.py:94
  268.2 6.6 %collective-permute-done = bf16[768,128]{0,1:T(8,128)(2,1)S(1)} collective-permute-done((bf16[768,128]{0,1:T(8,128)(2,1)S(1)}, bf16[768,128]{0,1:T(8,128)(2,1)S(1)}, u32[]{:S(2)}, u32[]{:S(2)}) %collective-permute-start) | collective-permute-done | bytes 196640 | tf_op jit(solution)/shard_map/ppermute | solution.py:24
  278.3 14.9 %fusion.27 = f32[768,512]{0,1:T(8,128)S(1)} fusion(bf16[8192,512]{1,0:T(8,128)(2,1)} %param.16, bf16[768,8192]{1,0:T(8,128)(2,1)} %all-gather.8.cloned.1.call-done, f32[8192]{0:T(1024)S(1)} %convert_element_type.74, f32[768]{0:T(1024)S(1)} %add_rsqrt_fusion), kind=kOutput, calls=%fused_computation.32 | convolution fusion | flops 6467616768 | bytes 22580224 | tf_op jit(solution)/shard_map/dot_general | solution.py:88
  295.0 29.2 %all-gather.10.cloned.1.call-done = bf16[6144,128]{0,1:T(8,128)(2,1)} async-done(((bf16[768,128]{0,1:T(8,128)(2,1)}), bf16[6144,128]{0,1:T(8,128)(2,1)}) %all-gather.10.cloned.1.call-update) | async-done | bytes 1572880 | tf_op jit(solution)/shard_map/all_gather | solution.py:119
  324.2 1.9 copy.22
  326.1 49.1 %all-gather.12.cloned.1.call-done = bf16[6144,1,128]{0,2,1:T(8,128)(2,1)} async-done(((bf16[768,1,128]{0,2,1:T(8,128)(2,1)}), bf16[6144,1,128]{0,2,1:T(8,128)(2,1)}) %all-gather.12.cloned.1.call-update) | async-done | bytes 1572880 | tf_op jit(solution)/shard_map/all_gather | solution.py:118
  375.2 2.6 copy.21
  379.0 125.1 %while.15 = (s32[]{:T(128)}, f32[3072]{0:T(1024)S(1)}, f32[3072]{0:T(1024)S(1)}, f32[3072,128]{1,0:T(8,128)}, s32[8]{0:T(128)S(1)}, /*index=5*/s32[]{:T(128)}, s...) while((s32[]{:T(128)}, f32[3072]{0:T(1024)S(1)}, ...), condition=%wide.region_14.15_spmd.clone, body=%wide.region_7.14_spmd.clone.sunk | while | flops 1260663552 | bytes 33017688 | solution.py:150
  380.3 14.4 %conditional.3 = ((f32[3072]{0:T(1024)S(1)}, f32[3072]{0:T(1024)S(1)}, f32[3072,128]{1,0:T(8,128)})) conditional(s32[]{:T(128)} %convert_element_type.210, (f32[3072]{0:T(1024)S(1)}, f32[3072]{0:T(1024)S(1)}, f32[3072,128]{1,0:T(8,128)}) %tuple.49, (s32[]{:T(128)}, s32[768]{0:T(1024)S(1)}, s32[3]{0:T(128)S(1)}, s32[768]{0:T(1024)S(1)}, ...), branch_computations={%region_8.8_spmd, %region_9.13_spmd} | conditional | flops 1260663552 | bytes 33017424 | solution.py:148
  382.0 3.5 fusion.4
  385.5 3.3 fusion.6
  388.8 5.8 %fusion.9 = f32[3072,128]{1,0:T(8,128)} fusion(f32[768,3072]{1,0:T(8,128)S(1)} %get-tuple-element.264, f32[3072]{0:T(1024)S(1)} %max.4, s32[3072]{0:T(1024)S(1)} %eq.13, s32[3072]{0:T(1024)S(1)} %le.23, s32[768]{0:T(1024)S(1)} %convert_reduce_fusion, s32[768]{0:T(1024)S(1)} %iota_add_fusion, f32[3072,128]{1,0:T(8,128)} %get-tuple-element.145, ...), kind=kOutput, calls=%fused_computation.9 | convolution fusion | flops 623640576 | bytes 12836868 | tf_op jit(solution)/shard_map/while/body/eval_jaxpr/cond/branch_1_fun/dot_general | solution.py:143
  395.9 14.4 %conditional.3 = ((f32[3072]{0:T(1024)S(1)}, f32[3072]{0:T(1024)S(1)}, f32[3072,128]{1,0:T(8,128)})) conditional(s32[]{:T(128)} %convert_element_type.210, (f32[3072]{0:T(1024)S(1)}, f32[3072]{0:T(1024)S(1)}, f32[3072,128]{1,0:T(8,128)}) %tuple.49, (s32[]{:T(128)}, s32[768]{0:T(1024)S(1)}, s32[3]{0:T(128)S(1)}, s32[768]{0:T(1024)S(1)}, ...), branch_computations={%region_8.8_spmd, %region_9.13_spmd} | conditional | flops 1260663552 | bytes 33017424 | solution.py:148
  397.6 3.5 fusion.4
  401.1 3.3 fusion.6
  404.5 5.8 %fusion.9 = f32[3072,128]{1,0:T(8,128)} fusion(f32[768,3072]{1,0:T(8,128)S(1)} %get-tuple-element.264, f32[3072]{0:T(1024)S(1)} %max.4, s32[3072]{0:T(1024)S(1)} %eq.13, s32[3072]{0:T(1024)S(1)} %le.23, s32[768]{0:T(1024)S(1)} %convert_reduce_fusion, s32[768]{0:T(1024)S(1)} %iota_add_fusion, f32[3072,128]{1,0:T(8,128)} %get-tuple-element.145, ...), kind=kOutput, calls=%fused_computation.9 | convolution fusion | flops 623640576 | bytes 12836868 | tf_op jit(solution)/shard_map/while/body/eval_jaxpr/cond/branch_1_fun/dot_general | solution.py:143
  411.5 14.4 %conditional.3 = ((f32[3072]{0:T(1024)S(1)}, f32[3072]{0:T(1024)S(1)}, f32[3072,128]{1,0:T(8,128)})) conditional(s32[]{:T(128)} %convert_element_type.210, (f32[3072]{0:T(1024)S(1)}, f32[3072]{0:T(1024)S(1)}, f32[3072,128]{1,0:T(8,128)}) %tuple.49, (s32[]{:T(128)}, s32[768]{0:T(1024)S(1)}, s32[3]{0:T(128)S(1)}, s32[768]{0:T(1024)S(1)}, ...), branch_computations={%region_8.8_spmd, %region_9.13_spmd} | conditional | flops 1260663552 | bytes 33017424 | solution.py:148
  413.2 3.5 fusion.4
  416.8 3.3 fusion.6
  420.1 5.8 %fusion.9 = f32[3072,128]{1,0:T(8,128)} fusion(f32[768,3072]{1,0:T(8,128)S(1)} %get-tuple-element.264, f32[3072]{0:T(1024)S(1)} %max.4, s32[3072]{0:T(1024)S(1)} %eq.13, s32[3072]{0:T(1024)S(1)} %le.23, s32[768]{0:T(1024)S(1)} %convert_reduce_fusion, s32[768]{0:T(1024)S(1)} %iota_add_fusion, f32[3072,128]{1,0:T(8,128)} %get-tuple-element.145, ...), kind=kOutput, calls=%fused_computation.9 | convolution fusion | flops 623640576 | bytes 12836868 | tf_op jit(solution)/shard_map/while/body/eval_jaxpr/cond/branch_1_fun/dot_general | solution.py:143
  427.2 14.4 %conditional.3 = ((f32[3072]{0:T(1024)S(1)}, f32[3072]{0:T(1024)S(1)}, f32[3072,128]{1,0:T(8,128)})) conditional(s32[]{:T(128)} %convert_element_type.210, (f32[3072]{0:T(1024)S(1)}, f32[3072]{0:T(1024)S(1)}, f32[3072,128]{1,0:T(8,128)}) %tuple.49, (s32[]{:T(128)}, s32[768]{0:T(1024)S(1)}, s32[3]{0:T(128)S(1)}, s32[768]{0:T(1024)S(1)}, ...), branch_computations={%region_8.8_spmd, %region_9.13_spmd} | conditional | flops 1260663552 | bytes 33017424 | solution.py:148
  428.9 3.5 fusion.4
  432.4 3.3 fusion.6
  435.7 5.8 %fusion.9 = f32[3072,128]{1,0:T(8,128)} fusion(f32[768,3072]{1,0:T(8,128)S(1)} %get-tuple-element.264, f32[3072]{0:T(1024)S(1)} %max.4, s32[3072]{0:T(1024)S(1)} %eq.13, s32[3072]{0:T(1024)S(1)} %le.23, s32[768]{0:T(1024)S(1)} %convert_reduce_fusion, s32[768]{0:T(1024)S(1)} %iota_add_fusion, f32[3072,128]{1,0:T(8,128)} %get-tuple-element.145, ...), kind=kOutput, calls=%fused_computation.9 | convolution fusion | flops 623640576 | bytes 12836868 | tf_op jit(solution)/shard_map/while/body/eval_jaxpr/cond/branch_1_fun/dot_general | solution.py:143
  442.8 14.4 %conditional.3 = ((f32[3072]{0:T(1024)S(1)}, f32[3072]{0:T(1024)S(1)}, f32[3072,128]{1,0:T(8,128)})) conditional(s32[]{:T(128)} %convert_element_type.210, (f32[3072]{0:T(1024)S(1)}, f32[3072]{0:T(1024)S(1)}, f32[3072,128]{1,0:T(8,128)}) %tuple.49, (s32[]{:T(128)}, s32[768]{0:T(1024)S(1)}, s32[3]{0:T(128)S(1)}, s32[768]{0:T(1024)S(1)}, ...), branch_computations={%region_8.8_spmd, %region_9.13_spmd} | conditional | flops 1260663552 | bytes 33017424 | solution.py:148
  444.5 3.5 fusion.4
  448.1 3.3 fusion.6
  451.4 5.8 %fusion.9 = f32[3072,128]{1,0:T(8,128)} fusion(f32[768,3072]{1,0:T(8,128)S(1)} %get-tuple-element.264, f32[3072]{0:T(1024)S(1)} %max.4, s32[3072]{0:T(1024)S(1)} %eq.13, s32[3072]{0:T(1024)S(1)} %le.23, s32[768]{0:T(1024)S(1)} %convert_reduce_fusion, s32[768]{0:T(1024)S(1)} %iota_add_fusion, f32[3072,128]{1,0:T(8,128)} %get-tuple-element.145, ...), kind=kOutput, calls=%fused_computation.9 | convolution fusion | flops 623640576 | bytes 12836868 | tf_op jit(solution)/shard_map/while/body/eval_jaxpr/cond/branch_1_fun/dot_general | solution.py:143
  458.5 14.4 %conditional.3 = ((f32[3072]{0:T(1024)S(1)}, f32[3072]{0:T(1024)S(1)}, f32[3072,128]{1,0:T(8,128)})) conditional(s32[]{:T(128)} %convert_element_type.210, (f32[3072]{0:T(1024)S(1)}, f32[3072]{0:T(1024)S(1)}, f32[3072,128]{1,0:T(8,128)}) %tuple.49, (s32[]{:T(128)}, s32[768]{0:T(1024)S(1)}, s32[3]{0:T(128)S(1)}, s32[768]{0:T(1024)S(1)}, ...), branch_computations={%region_8.8_spmd, %region_9.13_spmd} | conditional | flops 1260663552 | bytes 33017424 | solution.py:148
  460.2 3.5 fusion.4
  463.7 3.3 fusion.6
  467.0 5.8 %fusion.9 = f32[3072,128]{1,0:T(8,128)} fusion(f32[768,3072]{1,0:T(8,128)S(1)} %get-tuple-element.264, f32[3072]{0:T(1024)S(1)} %max.4, s32[3072]{0:T(1024)S(1)} %eq.13, s32[3072]{0:T(1024)S(1)} %le.23, s32[768]{0:T(1024)S(1)} %convert_reduce_fusion, s32[768]{0:T(1024)S(1)} %iota_add_fusion, f32[3072,128]{1,0:T(8,128)} %get-tuple-element.145, ...), kind=kOutput, calls=%fused_computation.9 | convolution fusion | flops 623640576 | bytes 12836868 | tf_op jit(solution)/shard_map/while/body/eval_jaxpr/cond/branch_1_fun/dot_general | solution.py:143
  474.1 14.4 %conditional.3 = ((f32[3072]{0:T(1024)S(1)}, f32[3072]{0:T(1024)S(1)}, f32[3072,128]{1,0:T(8,128)})) conditional(s32[]{:T(128)} %convert_element_type.210, (f32[3072]{0:T(1024)S(1)}, f32[3072]{0:T(1024)S(1)}, f32[3072,128]{1,0:T(8,128)}) %tuple.49, (s32[]{:T(128)}, s32[768]{0:T(1024)S(1)}, s32[3]{0:T(128)S(1)}, s32[768]{0:T(1024)S(1)}, ...), branch_computations={%region_8.8_spmd, %region_9.13_spmd} | conditional | flops 1260663552 | bytes 33017424 | solution.py:148
  475.8 3.5 fusion.4
  479.3 3.3 fusion.6
  482.6 5.8 %fusion.9 = f32[3072,128]{1,0:T(8,128)} fusion(f32[768,3072]{1,0:T(8,128)S(1)} %get-tuple-element.264, f32[3072]{0:T(1024)S(1)} %max.4, s32[3072]{0:T(1024)S(1)} %eq.13, s32[3072]{0:T(1024)S(1)} %le.23, s32[768]{0:T(1024)S(1)} %convert_reduce_fusion, s32[768]{0:T(1024)S(1)} %iota_add_fusion, f32[3072,128]{1,0:T(8,128)} %get-tuple-element.145, ...), kind=kOutput, calls=%fused_computation.9 | convolution fusion | flops 623640576 | bytes 12836868 | tf_op jit(solution)/shard_map/while/body/eval_jaxpr/cond/branch_1_fun/dot_general | solution.py:143
  489.7 14.4 %conditional.3 = ((f32[3072]{0:T(1024)S(1)}, f32[3072]{0:T(1024)S(1)}, f32[3072,128]{1,0:T(8,128)})) conditional(s32[]{:T(128)} %convert_element_type.210, (f32[3072]{0:T(1024)S(1)}, f32[3072]{0:T(1024)S(1)}, f32[3072,128]{1,0:T(8,128)}) %tuple.49, (s32[]{:T(128)}, s32[768]{0:T(1024)S(1)}, s32[3]{0:T(128)S(1)}, s32[768]{0:T(1024)S(1)}, ...), branch_computations={%region_8.8_spmd, %region_9.13_spmd} | conditional | flops 1260663552 | bytes 33017424 | solution.py:148
  491.4 3.5 fusion.4
  495.0 3.3 fusion.6
  498.3 5.8 %fusion.9 = f32[3072,128]{1,0:T(8,128)} fusion(f32[768,3072]{1,0:T(8,128)S(1)} %get-tuple-element.264, f32[3072]{0:T(1024)S(1)} %max.4, s32[3072]{0:T(1024)S(1)} %eq.13, s32[3072]{0:T(1024)S(1)} %le.23, s32[768]{0:T(1024)S(1)} %convert_reduce_fusion, s32[768]{0:T(1024)S(1)} %iota_add_fusion, f32[3072,128]{1,0:T(8,128)} %get-tuple-element.145, ...), kind=kOutput, calls=%fused_computation.9 | convolution fusion | flops 623640576 | bytes 12836868 | tf_op jit(solution)/shard_map/while/body/eval_jaxpr/cond/branch_1_fun/dot_general | solution.py:143
  504.1 2.0 divide_convert_fusion
  (138 shorter events, 27.6 us)
Async XLA Ops:
  6.5 251.3 %copy-start = (bf16[8192,128]{1,0:T(8,128)(2,1)S(1)}, bf16[8192,128]{1,0:T(8,128)(2,1)}, u32[]{:S(2)}) copy-start(bf16[8192,128]{1,0:T(8,128)(2,1)} %param.17) | copy-start | bytes 6291460
  6.5 108.0 %reduce-scatter.2.cloned.1.call-start = ((), (), s32[]{:S(2)}) async-start(), calls=%async_computation.1 | async-start | bytes 8912896 | tf_op jit(solution)/shard_map/reduce_scatter | solution.py:62
  16.7 99.6 %copy-start.3 = (s32[8]{0:T(128)S(1)}, s32[8]{0:T(128)}, u32[]{:S(2)}) copy-start(s32[8]{0:T(128)} %param.18) | copy-start | bytes 100
  16.8 158.4 %copy-start.2 = (bf16[8192]{0:T(1024)(128)(2,1)S(1)}, bf16[8192]{0:T(1024)(128)(2,1)}, u32[]{:S(2)}) copy-start(bf16[8192]{0:T(1024)(128)(2,1)} %param.15) | copy-start | bytes 49156
  16.8 153.8 %all-gather.6.cloned.1.call-start = ((), (), s32[]{:S(2)}) async-start(), calls=%async_computation.2 | async-start | bytes 2359296 | tf_op jit(solution)/shard_map/all_gather | solution.py:70
  116.3 134.5 %all-gather.8.cloned.1.call-start = ((), (), s32[]{:S(2)}) async-start(), calls=%async_computation.3 | async-start | bytes 13369344 | tf_op jit(solution)/shard_map/all_gather | solution.py:82
  175.1 149.1 %all-gather.10.cloned.1.call-start = ((), (), s32[]{:S(2)}) async-start(), calls=%async_computation.4 | async-start | bytes 1769472 | tf_op jit(solution)/shard_map/all_gather | solution.py:119
  257.9 17.7 %copy-start.4 = (s32[3]{0:T(128)S(1)}, s32[3]{0:T(128)}, u32[]{:S(2)}) copy-start(s32[3]{0:T(128)} %param.19) | copy-start | bytes 40
  266.9 7.8 %collective-permute-start = (bf16[768,128]{0,1:T(8,128)(2,1)S(1)}, bf16[768,128]{0,1:T(8,128)(2,1)S(1)}, u32[]{:S(2)}, u32[]{:S(2)}) collective-permute-start(bf16[768,128]{0,1:T(8,128)(2,1)S(1)} %fusion.39), channel_id=1, source_target_pairs={{0,1},{1,0},{2,3},{3,2},{4,5},{5,4},{6,7},{7,6},{8,9},{9,8},{10,11... | collective-permute-start | bytes 589832 | tf_op jit(solution)/shard_map/ppermute | solution.py:24
  275.5 99.7 %all-gather.12.cloned.1.call-start = ((), (), s32[]{:S(2)}) async-start(), calls=%async_computation.5 | async-start | bytes 1769472 | tf_op jit(solution)/shard_map/all_gather | solution.py:118
  504.1 3.4 copy-start.1
Sparse Core Ops, SparseCore 0:
  16.9 97.5 reduce-scatter.1
  116.8 53.6 all-gather.5
  175.2 75.5 all-gather.7
  275.6 48.5 all-gather.9
  326.5 48.6 all-gather.11
where the time goes:
time: 515 us; the launch traced here: 514 us
  waiting for transfers between devices  312 us (61%)
  matrix products  113 us (22%)
  other arithmetic  48.8 us (9%)
  local copies, waits for them, and re-layouts  19 us (4%)
  between operations  13.4 us (3%)
  loops' own time  5.84 us (1%)
    reduce_scatter x1, waiting for transfers between devices, shards(): lax.psum_scatter(lax.dot_general(proj_weight, activated, (((0,), (1,)), (...  97.7 us
    all_gather x1, waiting for transfers between devices, shards(): hidden = lax.all_gather(assembled, ('grp', 'tp'), axis=1, tiled=True)  75.6 us
    all_gather x1, waiting for transfers between devices, shards(): piece = lax.all_gather(my_share, 'ctx', axis=1, tiled=True)  54 us
    all_gather x1, waiting for transfers between devices, shards(): key_block = lax.all_gather(projected_key_rows, 'ctx', axis=0, tiled=True)  49.1 us
    dot_general x8, matrix products, update(): jnp.dot(weights.astype(jnp.bfloat16), values_here, preferred_element_type...  46.8 us
    all_gather x1, waiting for transfers between devices, shards(): lax.all_gather(projected_value_rows, 'ctx', axis=0, tiled=True)  29.2 us
    dot_general x8, matrix products, update(): lax.dot_general(queries, keys_here, (((1,), (1,)), ((), ())), preferred_e...  28.1 us
    reduce_sum x8, other arithmetic, update(): denom_sum = denom_sum * rescale + jnp.sum(weights, axis=1)  26.3 us
  transfers between devices with their start and end apart: 6, of which 6 were waited for; matrix products, arithmetic and copies ran while one was open for 4% of the time, Pallas kernels for 0%

commit v1 on v0

v1 whole, which is shorter than its diff:
```python
import functools
import math

import jax
import jax.numpy as jnp
from jax import lax
from jax.experimental import pallas as pl
from jax.experimental.pallas import tpu as pltpu
from jax.sharding import PartitionSpec as P

HEAD_WIDTH = 128
VTOK = 256
ROPE_BASE = 1000000.0
NORM_EPSILON = 1e-06
MASKED_SCORE = -1e30
QUERY_SCALE = math.log2(math.e) / math.sqrt(HEAD_WIDTH)
KEY_STEP = 512
QUERY_STEP = 256
VMEM_LIMIT = 56 * 1024 * 1024

F32 = jnp.float32
BF16 = jnp.bfloat16


def send_core(block):
    return lax.ppermute(block, "grp", [(i, i ^ 1) for i in range(4)])


def send_pair(block):
    return lax.ppermute(block, "grp", [(i, i ^ 2) for i in range(4)])


def send_z(block, shift):
    return lax.ppermute(block, "tp", [(i, (i + shift) % 4) for i in range(4)])


def send_z_pair(block):
    return lax.ppermute(block, "tp", [(i, i ^ 1) for i in range(4)])


def send_ctx_pair(block):
    return lax.ppermute(block, "ctx", [(i, i ^ 1) for i in range(8)])


def send_y(block, shift):
    return lax.ppermute(block, "ctx", [(i, (i + 2 * shift) % 8) for i in range(8)])


def gather_ring(own, pair, ring):
    other = pair(own)
    plus, minus, across = ring(own, 1), ring(own, 3), ring(own, 2)
    other_plus, other_minus = ring(other, 1), ring(other, 3)
    other_across = pair(across)
    return [[own, other], [plus, other_plus], [across, other_across], [minus, other_minus]]


def scatter_ring(parts):
    low = lambda value: value.astype(BF16)
    from_minus, from_plus = send_z(low(parts[1][1]), 1), send_z(low(parts[3][1]), 3)
    across = send_pair(low(parts[2][1]))
    last = [send_z(low(parts[1][0]), 1), send_z(low(parts[3][0]), 3)]
    last.append(send_z(low(parts[2][0] + across.astype(F32)), 2))
    last.append(
        send_pair(low(parts[0][1] + from_minus.astype(F32) + from_plus.astype(F32)))
    )
    return low(parts[0][0] + sum(piece.astype(F32) for piece in last))


def vmem_spec():
    return pl.BlockSpec(memory_space=pltpu.VMEM)


def smem_spec():
    return pl.BlockSpec(memory_space=pltpu.SMEM)


def params():
    return pltpu.CompilerParams(vmem_limit_bytes=VMEM_LIMIT)


def project_terms(activated, weight, blocks):
    rows, depth = activated.shape
    width = weight.shape[1] // 16

    def kernel(ids, act_ref, weight_ref, out_ref):
        out_ref[0] = jnp.dot(
            act_ref[...], weight_ref[...], preferred_element_type=F32
        ).astype(BF16)

    return pl.pallas_call(
        kernel,
        out_shape=jax.ShapeDtypeStruct((8, rows, width), BF16),
        grid_spec=pltpu.PrefetchScalarGridSpec(
            num_scalar_prefetch=1,
            grid=(8,),
            in_specs=[
                pl.BlockSpec((rows, depth), lambda i, ids: (0, 0)),
                pl.BlockSpec((depth, width), lambda i, ids: (0, ids[i])),
            ],
            out_specs=pl.BlockSpec((1, rows, width), lambda i, ids: (i, 0, 0)),
        ),
        compiler_params=params(),
        cost_estimate=pl.CostEstimate(
            flops=2 * rows * depth * 8 * width,
            bytes_accessed=2 * (rows * depth + depth * 8 * width + rows * 8 * width),
            transcendentals=0,
        ),
    )(blocks, activated, weight)


def rotate(values, cosine, sine):
    return values * cosine + pltpu.roll(values, HEAD_WIDTH // 2, 1) * sine


def project_rows(sources, order, turn, weights, gain, tables, inverse, kinds):
    steps_each = sources[0].shape[0]
    steps = steps_each * len(sources)
    slots, rows, width = sources[0].shape[1:]
    columns = [weight.shape[1] for weight in weights]
    count, wcount = len(sources), len(weights)
    make_inverse = inverse is None
    rotated = "q" in kinds

    def kernel(order_ref, turn_ref, *refs):
        refs = list(refs)
        source_refs = [refs.pop(0) for _ in range(count)]
        weight_refs = [refs.pop(0) for _ in range(wcount)]
        gain_ref = refs.pop(0)
        table_refs = [refs.pop(0) for _ in range(2)] if rotated else None
        inverse_ref = None if make_inverse else refs.pop(0)
        out_refs = [refs.pop(0) for _ in range(wcount)]
        inverse_out = refs.pop(0) if make_inverse else None
        totals = [refs.pop(0) for _ in range(wcount)]
        squares = refs.pop(0) if make_inverse else None
        step = pl.program_id(0)

        @pl.when(step == 0)
        def start():
            for total in totals:
                total[...] = jnp.zeros_like(total)
            if make_inverse:
                squares[...] = jnp.zeros_like(squares)

        def add(source_ref):
            for slot in range(slots):
                here = lax.rem(turn_ref[0] + turn_ref[1] * slot, slots)
                block = source_ref[0, here]
                if make_inverse:
                    wide = block.astype(F32)
                    square = wide * wide
                    sums = square[:, 0:128]
                    for lane in range(128, width, 128):
                        sums += square[:, lane : lane + 128]
                    squares[...] += sums
                scaled = block * gain_ref[0, slot : slot + 1]
                for weight_ref, total in zip(weight_refs, totals):
                    total[...] += jnp.dot(
                        scaled,
                        weight_ref[slot * width : (slot + 1) * width],
                        preferred_element_type=F32,
                    )

        if count == 1:
            add(source_refs[0])
        else:
            for place in range(count):
                pl.when(step // steps_each == place)(
                    functools.partial(add, source_refs[place])
                )

        @pl.when(step == steps - 1)
        def finish():
            if make_inverse:
                mean = jnp.sum(squares[...], axis=1, keepdims=True) / (steps * slots * width)
                scale = jnp.broadcast_to(lax.rsqrt(mean + NORM_EPSILON), (rows, 128))
                inverse_out[...] = scale
            else:
                scale = inverse_ref[...]
            for kind, total, out_ref in zip(kinds, totals, out_refs):
                for lane in range(0, total.shape[1], 128):
                    value = total[:, lane : lane + 128] * scale
                    if kind == "q":
                        value = rotate(value, table_refs[0][...], table_refs[1][...])
                        value = value * QUERY_SCALE
                    out_ref[:, lane : lane + 128] = value.astype(BF16)

    def source_spec(place):
        def index(i, order_ref, turn_ref):
            return (jnp.clip(i - place * steps_each, 0, steps_each - 1), 0, 0, 0)

        return pl.BlockSpec((1, slots, rows, width), index)

    in_specs = [source_spec(place) for place in range(count)]
    in_specs += [
        pl.BlockSpec((slots * width, size), lambda i, order_ref, turn_ref: (order_ref[i], 0))
        for size in columns
    ]
    in_specs.append(
        pl.BlockSpec((1, slots, width), lambda i, order_ref, turn_ref: (order_ref[i], 0, 0))
    )
    operands = list(sources) + list(weights) + [gain.reshape(steps, slots, width)]
    whole = lambda i, order_ref, turn_ref: (0, 0)
    if rotated:
        in_specs += [pl.BlockSpec((rows, 128), whole)] * 2
        operands += list(tables)
    if not make_inverse:
        in_specs.append(pl.BlockSpec((rows, 128), whole))
        operands.append(inverse)
    out_shape = [jax.ShapeDtypeStruct((rows, size), BF16) for size in columns]
    out_specs = [pl.BlockSpec((rows, size), whole) for size in columns]
    scratch = [pltpu.VMEM((rows, size), F32) for size in columns]
    if make_inverse:
        out_shape.append(jax.ShapeDtypeStruct((rows, 128), F32))
        out_specs.append(pl.BlockSpec((rows, 128), whole))
        scratch.append(pltpu.VMEM((rows, 128), F32))
    depth = steps * slots * width
    return pl.pallas_call(
        kernel,
        out_shape=out_shape,
        grid_spec=pltpu.PrefetchScalarGridSpec(
            num_scalar_prefetch=2,
            grid=(steps,),
            in_specs=in_specs,
            out_specs=out_specs,
            scratch_shapes=scratch,
        ),
        compiler_params=params(),
        cost_estimate=pl.CostEstimate(
            flops=2 * rows * depth * sum(columns),
            bytes_accessed=2 * depth * (rows + sum(columns)),
            transcendentals=0,
        ),
    )(order, turn, *operands)


def join_halves(own, partner, tables, parity, queries=None):
    rows = own.shape[0]
    width = 256 if queries is None else 256 + queries.shape[1]
    lead = width - 256

    def kernel(parity_ref, *refs):
        refs = list(refs)
        own_ref, partner_ref, cosine_ref, sine_ref = refs[:4]
        out_ref = refs[-1]
        if lead:
            out_ref[:, :lead] = refs[4][...]
        first = parity_ref[0] == 0
        own_wide, partner_wide = own_ref[...].astype(F32), partner_ref[...].astype(F32)
        lower = jnp.where(first, own_wide, partner_wide)
        upper = jnp.where(first, partner_wide, own_wide)
        left = lax.broadcasted_iota(jnp.int32, (rows, 128), 1) < 64
        keys = jnp.where(left, lower, pltpu.roll(upper, 64, 1))
        values = jnp.where(left, pltpu.roll(lower, 64, 1), upper)
        keys = rotate(keys, cosine_ref[...], sine_ref[...])
        out_ref[:, lead : lead + 128] = keys.astype(BF16)
        out_ref[:, lead + 128 :] = values.astype(BF16)

    operands = [own, partner, *tables] + ([] if queries is None else [queries])
    return pl.pallas_call(
        kernel,
        out_shape=jax.ShapeDtypeStruct((rows, width), BF16),
        in_specs=[smem_spec()] + [vmem_spec()] * len(operands),
        out_specs=vmem_spec(),
        compiler_params=params(),
        cost_estimate=pl.CostEstimate(
            flops=rows * 1024, bytes_accessed=rows * width * 8, transcendentals=0
        ),
    )(parity, *operands)


def attend(facts, queries, text, visual):
    rows, width = queries.shape
    heads = width // HEAD_WIDTH
    total_rows = rows * len(text)
    pieces = len(text)

    def kernel(facts_ref, q_ref, *refs):
        refs = list(refs)
        text_refs = [refs.pop(0) for _ in range(pieces)]
        visual_refs = [refs.pop(0) for _ in range(pieces)]
        out_ref, wide_kv, wide_q, key_ref, value_ref, query_ref, total_ref, most_ref = refs
        offset, end_0, end_1 = facts_ref[0], facts_ref[1], facts_ref[2]

        def store_rows(target, start, values):
            group, shift = start // 8, lax.rem(start, 8)
            count = VTOK // 8
            turned = pltpu.roll(values.reshape(count, 8, values.shape[1]), shift, 1)
            early = lax.broadcasted_iota(jnp.int32, (1, 8, values.shape[1]), 1) < shift
            target[pl.ds(group, 1)] = jnp.where(early, target[pl.ds(group, 1)], turned[:1])
            target[pl.ds(group + 1, count - 1)] = jnp.where(early, turned[:-1], turned[1:])
            end = pl.ds(group + count, 1)
            target[end] = jnp.where(early, turned[-1:], target[end])

        grouped = lambda values: values.astype(F32).reshape(-1, 8, values.shape[1])
        wide_q[VTOK // 8 : (VTOK + rows) // 8] = grouped(q_ref[...])
        for piece, text_ref in enumerate(text_refs):
            wide_kv[pl.ds(facts_ref[3 + piece] * (rows // 8), rows // 8)] = grouped(text_ref[...])
        for piece, visual_ref in enumerate(visual_refs):
            start = facts_ref[3 + pieces + piece]
            store_rows(wide_kv, start, visual_ref[:, width:].astype(F32))
            local = jnp.clip(start - offset + VTOK, 0, rows + VTOK)

            @pl.when((local > 0) & (local < rows + VTOK))
            def place(visual_ref=visual_ref, local=local):
                store_rows(wide_q, local, visual_ref[:, :width].astype(F32))

        def narrow(step, carry):
            span = pl.ds(pl.multiple_of(step * 256, 256), 256)
            both = wide_kv[pl.ds(step * 32, 32)].reshape(256, 256)
            key_ref[span] = both[:, :128].astype(BF16)
            value_ref[span, :128] = both[:, 128:].astype(BF16)
            value_ref[span, 128:] = jnp.ones((256, 128), BF16)
            return carry

        lax.fori_loop(0, total_rows // 256, narrow, 0)
        for head in range(heads):
            query_ref[head] = (
                wide_q[VTOK // 8 : (VTOK + rows) // 8, :, head * 128 : (head + 1) * 128]
                .reshape(rows, 128)
                .astype(BF16)
            )

        def doc_begin(position):
            return jnp.where(position >= end_1, end_1, jnp.where(position >= end_0, end_0, 0))

        def query_block(block, carry):
            base = pl.multiple_of(block * QUERY_STEP, QUERY_STEP)
            first = offset + base
            last = first + QUERY_STEP - 1
            low = doc_begin(first) // KEY_STEP
            high = last // KEY_STEP + 1
            clear_low = jnp.clip((doc_begin(last) + KEY_STEP - 1) // KEY_STEP, low, high)
            clear_high = jnp.clip((first + 1) // KEY_STEP, clear_low, high)
            total_ref[...] = jnp.zeros_like(total_ref)
            most_ref[...] = jnp.full_like(most_ref, MASKED_SCORE)

            def key_block(masked, index, carry):
                start = pl.multiple_of(index * KEY_STEP, KEY_STEP)
                keys = key_ref[pl.ds(start, KEY_STEP)]
                values = value_ref[pl.ds(start, KEY_STEP)]
                if masked:
                    shape = (QUERY_STEP, KEY_STEP)
                    row = first + lax.broadcasted_iota(jnp.int32, shape, 0)
                    key = start + lax.broadcasted_iota(jnp.int32, shape, 1)
                    allowed = (key <= row) & (key >= doc_begin(row))
                for head in range(heads):
                    scores = lax.dot_general(
                        query_ref[head, pl.ds(base, QUERY_STEP)],
                        keys,
                        (((1,), (1,)), ((), ())),
                        preferred_element_type=F32,
                    )
                    if masked:
                        scores = jnp.where(allowed, scores, MASKED_SCORE)
                    before = most_ref[head]
                    most = jnp.maximum(before, jnp.max(scores, axis=1, keepdims=True))
                    most_ref[head] = most
                    shrink = jnp.exp2(before - most)
                    weights = jnp.exp2(
                        scores - jnp.concatenate([most] * (KEY_STEP // 128), axis=1)
                    ).astype(BF16)
                    total_ref[head] = total_ref[head] * jnp.concatenate(
                        [shrink, shrink], axis=1
                    ) + jnp.dot(weights, values, preferred_element_type=F32)
                return carry

            lax.fori_loop(low, clear_low, functools.partial(key_block, True), 0)
            lax.fori_loop(clear_low, clear_high, functools.partial(key_block, False), 0)
            lax.fori_loop(clear_high, high, functools.partial(key_block, True), 0)
            for head in range(heads):
                result = total_ref[head, :, :128] / total_ref[head, :, 128:]
                out_ref[pl.ds(base, QUERY_STEP), head * 128 : (head + 1) * 128] = result.astype(
                    BF16
                )
            return carry

        lax.fori_loop(0, rows // QUERY_STEP, query_block, 0)

    return pl.pallas_call(
        kernel,
        out_shape=jax.ShapeDtypeStruct((rows, width), BF16),
        in_specs=[smem_spec()] + [vmem_spec()] * (1 + 2 * pieces),
        out_specs=vmem_spec(),
        scratch_shapes=[
            pltpu.VMEM((total_rows // 8 + 1, 8, 256), F32),
            pltpu.VMEM((rows // 8 + 2 * VTOK // 8 + 1, 8, width), F32),
            pltpu.VMEM((total_rows, 128), BF16),
            pltpu.VMEM((total_rows, 256), BF16),
            pltpu.VMEM((heads, rows, 128), BF16),
            pltpu.VMEM((heads, QUERY_STEP, 256), F32),
            pltpu.VMEM((heads, QUERY_STEP, 128), F32),
        ],
        compiler_params=params(),
        cost_estimate=pl.CostEstimate(
            flops=4 * rows * heads * 3000 * 128,
            bytes_accessed=8 * 2**20,
            transcendentals=rows * heads * 3000,
        ),
    )(facts, queries, *text, *visual)


def rotary_tables(prompt_lengths, positions):
    ends = jnp.cumsum(prompt_lengths)
    begin = jnp.where(
        positions >= ends[1], ends[1], jnp.where(positions >= ends[0], ends[0], 0)
    )
    half = HEAD_WIDTH // 2
    frequency = ROPE_BASE ** (-2.0 * jnp.arange(half, dtype=F32) / HEAD_WIDTH)
    angles = (positions - begin).astype(F32)[:, None] * frequency[None, :]
    cosine, sine = jnp.cos(angles), jnp.sin(angles)
    return (
        jnp.concatenate([cosine, cosine], axis=1),
        jnp.concatenate([-sine, sine], axis=1),
    )


def shards(
    enc_pre, proj_weight, prompt_hidden, norm_gain, q_weight, kv_weight, tile_starts, prompt_lengths
):
    rows, width = prompt_hidden.shape
    ctx, z, grp = lax.axis_index("ctx"), lax.axis_index("tp"), lax.axis_index("grp")
    half, core = grp // 2, grp % 2
    parity = (z % 2).reshape(1)
    offset = ctx * rows

    with jax.named_scope("text_gather"):
        text = lax.all_gather(prompt_hidden, ("grp", "tp"), axis=0, tiled=False)
        text = text.reshape(4, 4, rows, width)

    with jax.named_scope("tables"):
        text_tables = rotary_tables(prompt_lengths, offset + jnp.arange(rows, dtype=jnp.int32))
        here = jnp.sum(jnp.where(jnp.arange(8) == ctx, tile_starts, 0))
        visual_tables = rotary_tables(prompt_lengths, here + jnp.arange(VTOK, dtype=jnp.int32))

    with jax.named_scope("projector"):
        activated = jax.nn.gelu(enc_pre.astype(F32), approximate=False).astype(BF16)
        ahead = jnp.arange(8, dtype=jnp.int32)
        place = lambda which: ((half ^ (ahead % 2)) * 2 + which) * 4 + (z + ahead // 2) % 4
        theirs = project_terms(activated, proj_weight, place(1 - core))
        received = send_core(theirs)
        mine = project_terms(activated, proj_weight, place(core))
        parts = [
            [mine[2 * d + e].astype(F32) + received[2 * d + e].astype(F32) for e in range(2)]
            for d in range(4)
        ]
        visual = scatter_ring(parts)

    with jax.named_scope("visual_gather"):
        blocks = gather_ring(visual, send_pair, send_z)
        mine = jnp.stack([blocks[d][e] for e in range(2) for d in range(4)]).reshape(
            2, 4, VTOK, width
        )
        sibling = send_core(mine)

    gain = norm_gain.astype(BF16)
    with jax.named_scope("visual_rows"):
        order = jnp.stack(
            [(half ^ e) * 2 + (core ^ k) for k in range(2) for e in range(2)]
        ).astype(jnp.int32)
        turn = jnp.stack([z, jnp.int32(3)]).astype(jnp.int32)
        visual_q, visual_half, _ = project_rows(
            [mine, sibling], order, turn, [q_weight, kv_weight], gain, visual_tables, None,
            ["q", "kv"],
        )
        visual_partner = send_z_pair(visual_half)
        visual_all = join_halves(visual_half, visual_partner, visual_tables, parity, visual_q)
        visual_blocks = gather_ring(visual_all, send_ctx_pair, send_y)

    with jax.named_scope("text_rows"):
        order = jnp.arange(4, dtype=jnp.int32)
        turn = jnp.array([0, 1], jnp.int32)
        text_half, inverse = project_rows(
            [text], order, turn, [kv_weight], gain, None, None, ["kv"]
        )
        text_partner = send_z_pair(text_half)
        text_kv = join_halves(text_half, text_partner, text_tables, parity)
        text_blocks = gather_ring(text_kv, send_ctx_pair, send_y)
        (text_q,) = project_rows(
            [text], order, turn, [q_weight], gain, text_tables, inverse, ["q"]
        )

    with jax.named_scope("attention"):
        numbers = jnp.stack(
            [((ctx // 2 + 4 - d) % 4) * 2 + (ctx % 2) ^ e for d in range(4) for e in range(2)]
        ).astype(jnp.int32)
        picked = numbers[:, None] == jnp.arange(8, dtype=jnp.int32)[None, :]
        starts = jnp.sum(jnp.where(picked, tile_starts[None, :], 0), axis=1)
        ends = jnp.cumsum(prompt_lengths)
        facts = jnp.concatenate(
            [jnp.stack([offset, ends[0], ends[1]]), numbers, starts]
        ).astype(jnp.int32)
        flat = lambda blocks: [blocks[d][e] for d in range(4) for e in range(2)]
        return attend(facts, text_q, flat(text_blocks), flat(visual_blocks))


def solution(mesh):
    in_specs = (
        P("ctx", ("grp", "tp")),
        P(("grp", "tp"), None),
        P("ctx", ("grp", "tp")),
        P(),
        P(None, ("grp", "tp")),
        P(None, ("grp", "tp")),
        P(),
        P(),
    )
    out_specs = P("ctx", ("grp", "tp"))
    return jax.shard_map(shards, mesh=mesh, in_specs=in_specs, out_specs=out_specs, check_vma=False)
```

time: 515 us -> 224 us (0.43)
  waiting for transfers between devices: 312 us -> 56.3 us
  matrix products: 113 us -> 0 us
  Pallas kernels: 0 us -> 83.6 us
  starting transfers between devices: 1.43 us -> 43.9 us
  other arithmetic: 48.8 us -> 17.4 us
  local copies, waits for them, and re-layouts: 19 us -> 8.46 us
  loops' own time: 5.84 us -> 0 us
    all_gather x4 -> x1, waiting for transfers between devices: 208 us -> 0.01 us  [shards(): text = lax.all_gather(prompt_hidden, ('grp', 'tp'), axis=0, tiled=False)]
    dot_general x20 -> x0, matrix products: 113 us -> none  [the longest x8 46.8 us: update(): jnp.dot(weights.astype(jnp.bfloat16), values_here, preferred_element_type...]
    reduce_scatter x1 -> x0, waiting for transfers between devices: 97.7 us -> none  [shards(): lax.psum_scatter(lax.dot_general(proj_weight, activated, (((0,), (1,)), (...]
    pallas_call x0 -> x8, Pallas kernels: none -> 83.6 us  [the longest x3 32.1 us: project_rows(): pl.pallas_call(kernel, out_shape=out_shape, grid_spec=pltpu.PrefetchScala...]
    ppermute x1 -> x32, waiting for transfers between devices: 6.58 us -> 55.6 us  [the longest x10 26 us: send_z(): return lax.ppermute(block, 'tp', [(i, (i + shift) % 4) for i in range(4)])]
    ppermute x1 -> x32, starting transfers between devices: 1.26 us -> 43.9 us  [the longest x10 17 us: send_z(): return lax.ppermute(block, 'tp', [(i, (i + shift) % 4) for i in range(4)])]
    reduce_sum x20 -> x2, other arithmetic: 34.3 us -> 0.82 us  [the longest x1 0.63 us: shards(): here = jnp.sum(jnp.where(jnp.arange(8) == ctx, tile_starts, 0))]
    another operation x9 -> x0, loops' own time: 5.84 us -> none  [the longest x1 5.23 us: shards(): lax.scan(key_step, initial, (key_split, value_split, firsts))]
  transfers between devices with their start and end apart: 6 -> 33, of which waited for: 6 -> 15; matrix products, arithmetic and copies ran while one was open for 4% -> 10% of each run, Pallas kernels for 0% -> 23%
where the time goes in v1:
time: 224 us; the launch traced here: 223 us
  Pallas kernels  83.6 us (37%)
  waiting for transfers between devices  56.3 us (25%)
  starting transfers between devices  43.9 us (20%)
  other arithmetic  17.4 us (8%)
  between operations  13.8 us (6%)
  local copies, waits for them, and re-layouts  8.46 us (4%)
    pallas_call x3, Pallas kernels, project_rows(): pl.pallas_call(kernel, out_shape=out_shape, grid_spec=pltpu.PrefetchScala...  32.1 us
    pallas_call x1, Pallas kernels, attend(): pl.pallas_call(kernel, out_shape=jax.ShapeDtypeStruct((rows, width), BF16...  31.3 us
    ppermute x10, waiting for transfers between devices, send_z(): return lax.ppermute(block, 'tp', [(i, (i + shift) % 4) for i in range(4)])  26 us
    ppermute x10, starting transfers between devices, send_z(): return lax.ppermute(block, 'tp', [(i, (i + shift) % 4) for i in range(4)])  17 us
    pallas_call x2, Pallas kernels, project_terms(): pl.pallas_call(kernel, out_shape=jax.ShapeDtypeStruct((8, rows, width), B...  15.8 us
    ppermute x4, waiting for transfers between devices, send_pair(): return lax.ppermute(block, 'grp', [(i, i ^ 2) for i in range(4)])  12.9 us
    ppermute x10, starting transfers between devices, send_y(): lax.ppermute(block, 'ctx', [(i, (i + 2 * shift) % 8) for i in range(8)])  10.9 us
    ppermute x10, waiting for transfers between devices, send_y(): lax.ppermute(block, 'ctx', [(i, (i + 2 * shift) % 8) for i in range(8)])  7.66 us
  transfers between devices with their start and end apart: 33, of which 15 were waited for; matrix products, arithmetic and copies ran while one was open for 10% of the time, Pallas kernels for 23%

profile of v1, /device:TPU:30, one launch (start us, length us, event | category | flops | bytes accessed | tf_op | source)
XLA Modules:
  0.0 223.5 jit_solution(3204806650577435701)
XLA Ops:
  7.8 2.8 %fusion.1.act_ref = bf16[256,512]{1,0:T(8,128)(2,1)} fusion(bf16[256,512]{1,0:T(8,128)(2,1)} %param.9), kind=kLoop, calls=%fused_computation.6 | loop fusion | flops 8650752 | bytes 524288 | tf_op jit(solution)/shard_map/projector/convert_element_type | solution.py:436
  10.6 7.9 %projector.3 = bf16[8,256,512]{2,1,0:T(8,128)(2,1)} custom-call(s32[8]{0:T(128)} %multiply_add_fusion.ids, bf16[256,512]{1,0:T(8,128)(2,1)} %fusion.1.act_ref, bf16[512,8192]{1,0:T(8,128)(2,1)} %weight_ref.3), custom_call_target="tpu_custom_call" | custom-call | flops 1073741824 | bytes 6553600 | tf_op jit(solution)/shard_map/projector/pallas_call | solution.py:90
  19.1 8.0 %projector.2 = bf16[8,256,512]{2,1,0:T(8,128)(2,1)} custom-call(s32[8]{0:T(128)} %multiply_add_fusion.1.ids, bf16[256,512]{1,0:T(8,128)(2,1)} %fusion.1.act_ref, bf16[512,8192]{1,0:T(8,128)(2,1)} %weight_ref.3), custom_call_target="tpu_custom_call" | custom-call | flops 1073741824 | bytes 6553600 | tf_op jit(solution)/shard_map/projector/pallas_call | solution.py:90
  27.1 1.7 fusion.35
  29.6 4.0 %collective-permute-start.14 = (bf16[256,512]{1,0:T(8,128)(2,1)S(1)}, bf16[256,512]{1,0:T(8,128)(2,1)S(1)}, u32[]{:S(2)}, u32[]{:S(2)}) collective-permute-start(bf16[256,512]{1,0:T(8,128)(2,1)S(1)} %get-tuple-element.16), channel_id=1, source_target_pairs={{0,3},{1,0},{2,1},{3,2},{4,7},{5,4},{6,5},{7,6},{8,11},{9,8},{10,9... | collective-permute-start | bytes 786440 | tf_op jit(solution)/shard_map/projector/ppermute | solution.py:34
  33.6 3.2 %collective-permute-start.10 = (bf16[256,512]{1,0:T(8,128)(2,1)S(1)}, bf16[256,512]{1,0:T(8,128)(2,1)S(1)}, u32[]{:S(2)}, u32[]{:S(2)}) collective-permute-start(bf16[256,512]{1,0:T(8,128)(2,1)S(1)} %get-tuple-element.19), channel_id=1, source_target_pairs={{0,3},{1,0},{2,1},{3,2},{4,7},{5,4},{6,5},{7,6},{8,11},{9,8},{10,9... | collective-permute-start | bytes 786440 | tf_op jit(solution)/shard_map/projector/ppermute | solution.py:34
  36.8 3.7 %collective-permute-done.11 = bf16[256,512]{1,0:T(8,128)(2,1)S(1)} collective-permute-done((bf16[256,512]{1,0:T(8,128)(2,1)S(1)}, bf16[256,512]{1,0:T(8,128)(2,1)S(1)}, u32[]{:S(2)}, u32[]{:S(2)}) %collective-permute-start.11) | collective-permute-done | bytes 262176 | tf_op jit(solution)/shard_map/projector/ppermute | solution.py:30
  41.6 2.4 %collective-permute-done.13 = bf16[256,512]{1,0:T(8,128)(2,1)S(1)} collective-permute-done((bf16[256,512]{1,0:T(8,128)(2,1)S(1)}, bf16[256,512]{1,0:T(8,128)(2,1)S(1)}, u32[]{:S(2)}, u32[]{:S(2)}) %collective-permute-start.13) | collective-permute-done | bytes 262176 | tf_op jit(solution)/shard_map/projector/ppermute | solution.py:34
  44.0 1.3 fusion.33
  45.2 1.3 collective-permute-start.15
  46.6 1.5 collective-permute-start.12
  48.1 1.9 collective-permute-done.10
  50.0 1.5 collective-permute-done.9
  51.5 4.4 %collective-permute-done.15 = bf16[256,512]{1,0:T(8,128)(2,1)S(1)} collective-permute-done((bf16[256,512]{1,0:T(8,128)(2,1)S(1)}, bf16[256,512]{1,0:T(8,128)(2,1)S(1)}, u32[]{:S(2)}, u32[]{:S(2)}) %collective-permute-start.15) | collective-permute-done | bytes 262176 | tf_op jit(solution)/shard_map/projector/ppermute | solution.py:30
  55.9 5.9 %collective-permute-done.12 = bf16[256,512]{1,0:T(8,128)(2,1)S(1)} collective-permute-done((bf16[256,512]{1,0:T(8,128)(2,1)S(1)}, bf16[256,512]{1,0:T(8,128)(2,1)S(1)}, u32[]{:S(2)}, u32[]{:S(2)}) %collective-permute-start.12) | collective-permute-done | bytes 262176 | tf_op jit(solution)/shard_map/projector/ppermute | solution.py:34
  61.8 1.2 bitcast_dynamic-update-slice_fusion.7
  63.0 1.3 collective-permute-start.19
  64.3 1.8 collective-permute-start.17
  66.1 3.2 %collective-permute-start.18 = (bf16[256,512]{1,0:T(8,128)(2,1)S(1)}, bf16[256,512]{1,0:T(8,128)(2,1)S(1)}, u32[]{:S(2)}, u32[]{:S(2)}) collective-permute-start(bf16[256,512]{1,0:T(8,128)(2,1)S(1)} %get-tuple-element.14), channel_id=1, source_target_pairs={{0,3},{1,0},{2,1},{3,2},{4,7},{5,4},{6,5},{7,6},{8,11},{9,8},{10,9... | collective-permute-start | bytes 786440 | tf_op jit(solution)/shard_map/visual_gather/ppermute | solution.py:34
  69.3 4.8 %collective-permute-done.19 = bf16[256,512]{1,0:T(8,128)(2,1)S(1)} collective-permute-done((bf16[256,512]{1,0:T(8,128)(2,1)S(1)}, bf16[256,512]{1,0:T(8,128)(2,1)S(1)}, u32[]{:S(2)}, u32[]{:S(2)}) %collective-permute-start.19) | collective-permute-done | bytes 262176 | tf_op jit(solution)/shard_map/visual_gather/ppermute | solution.py:30
  74.1 3.2 %collective-permute-start.22 = (bf16[256,512]{1,0:T(8,128)(2,1)S(1)}, bf16[256,512]{1,0:T(8,128)(2,1)S(1)}, u32[]{:S(2)}, u32[]{:S(2)}) collective-permute-start(bf16[256,512]{1,0:T(8,128)(2,1)S(1)} %collective-permute-done.19), channel_id=1, source_target_pairs={{0,3},{1,0},{2,1},{3,2},{4,7},{5,4},{6,5},{7,6},{8,11},{9,8},{10,9... | collective-permute-start | bytes 786440 | tf_op jit(solution)/shard_map/visual_gather/ppermute | solution.py:34
  78.5 5.4 %collective-permute-done.16 = bf16[256,512]{1,0:T(8,128)(2,1)S(1)} collective-permute-done((bf16[256,512]{1,0:T(8,128)(2,1)S(1)}, bf16[256,512]{1,0:T(8,128)(2,1)S(1)}, u32[]{:S(2)}, u32[]{:S(2)}) %collective-permute-start.16) | collective-permute-done | bytes 262176 | tf_op jit(solution)/shard_map/visual_gather/ppermute | solution.py:34
  84.1 7.4 %collective-permute-done.20 = bf16[256,512]{1,0:T(8,128)(2,1)S(1)} collective-permute-done((bf16[256,512]{1,0:T(8,128)(2,1)S(1)}, bf16[256,512]{1,0:T(8,128)(2,1)S(1)}, u32[]{:S(2)}, u32[]{:S(2)}) %collective-permute-start.20) | collective-permute-done | bytes 262176 | tf_op jit(solution)/shard_map/visual_gather/ppermute | solution.py:34
  95.4 1.9 fusion.45
  98.6 9.9 %visual_rows.2 = (bf16[256,512]{1,0:T(8,128)(2,1)}, bf16[256,128]{1,0:T(8,128)(2,1)}, f32[256,128]{1,0:T(8,128)}) custom-call(s32[4]{0:T(128)} %pad_add_fusion.order_ref, s32[2]{0:T(128)} %pad_add_fusion.1.turn_ref, bf16[2,4,256,512]{3,2,1,0:T(8,128)(2,1)} %bitcast.66, bf16[2,4,256,512]{3,2,1,0:T(8,128)(2,1)} %collective-permute-done.23.refs_1_, ...), custom_call_target="tpu_custom_call" | custom-call | flops 2684354560 | bytes 14680064 | tf_op jit(solution)/shard_map/visual_rows/pallas_call | solution.py:217
  108.5 2.5 %collective-permute-start.24 = (bf16[256,128]{1,0:T(8,128)(2,1)}, bf16[256,128]{1,0:T(8,128)(2,1)S(1)}, u32[]{:S(2)}, u32[]{:S(2)}) collective-permute-start(bf16[256,128]{1,0:T(8,128)(2,1)} %get-tuple-element.11.refs_0_), channel_id=1, source_target_pairs={{0,1},{1,0},{2,3},{3,2},{4,5},{5,4},{6,7},{7,6},{8,9},{9,8},{10,11... | collective-permute-start | bytes 196616 | tf_op jit(solution)/shard_map/visual_rows/ppermute | solution.py:38
  111.0 1.2 subtract_convert_fusion
  112.2 2.4 %collective-permute-done.24.refs_1_ = bf16[256,128]{1,0:T(8,128)(2,1)S(1)} collective-permute-done((bf16[256,128]{1,0:T(8,128)(2,1)}, bf16[256,128]{1,0:T(8,128)(2,1)S(1)}, u32[]{:S(2)}, u32[]{:S(2)}) %collective-permute-start.24) | collective-permute-done | bytes 65568 | tf_op jit(solution)/shard_map/visual_rows/ppermute | solution.py:38
  115.2 2.1 visual_rows.3.refs_8_
  117.3 1.3 collective-permute-start.25
  118.9 2.6 %collective-permute-start.28 = (bf16[256,768]{1,0:T(8,128)(2,1)}, bf16[256,768]{1,0:T(8,128)(2,1)S(1)}, u32[]{:S(2)}, u32[]{:S(2)}) collective-permute-start(bf16[256,768]{1,0:T(8,128)(2,1)} %visual_rows.3.refs_8_), channel_id=1, source_target_pairs={{0,16},{4,20},{8,24},{12,28},{16,0},{20,4},{24,8},{28,12},{1,17},{... | collective-permute-start | bytes 1179656 | tf_op jit(solution)/shard_map/visual_rows/ppermute | solution.py:46
  122.5 9.2 %text_rows.3 = (bf16[768,128]{1,0:T(8,128)(2,1)}, f32[768,128]{1,0:T(8,128)}) custom-call(s32[4]{0:T(128)} %iota.39.order_ref, s32[2]{0:T(128)} %call_exported.0.turn_ref, bf16[4,4,768,512]{3,2,1,0:T(8,128)(2,1)} %bitcast.63, bf16[8192,128]{1,0:T(8,128)(2,1)} %refs_3_.1, bf16[4,4,512]{2,1,0:T(4,128)(2,1)} %reshape.80.refs_2_.refs_4_), custom_call_target="tpu_custom_call" | custom-call | flops 1610612736 | bytes 14680064 | tf_op jit(solution)/shard_map/text_rows/pallas_call | solution.py:217
  131.7 1.9 collective-permute-start
  133.6 1.4 fusion.40
  135.1 1.2 pad_maximum_fusion
  136.2 3.2 %collective-permute-start.27 = (bf16[256,768]{1,0:T(8,128)(2,1)S(1)}, bf16[256,768]{1,0:T(8,128)(2,1)S(1)}, u32[]{:S(2)}, u32[]{:S(2)}) collective-permute-start(bf16[256,768]{1,0:T(8,128)(2,1)S(1)} %collective-permute-done.25.refs_9_), channel_id=1, source_target_pairs={{0,8},{4,12},{8,16},{12,20},{16,24},{20,28},{24,0},{28,4},{1,9},{5... | collective-permute-start | bytes 1179656 | tf_op jit(solution)/shard_map/visual_rows/ppermute | solution.py:46
  139.5 2.2 collective-permute-start.29
  142.3 2.3 %text_rows.5.refs_0_ = bf16[768,256]{1,0:T(8,128)(2,1)} custom-call(s32[1]{0:T(128)} %bitcast.15.parity_ref, bf16[768,128]{1,0:T(8,128)(2,1)} %get-tuple-element.10.refs_0_, bf16[768,128]{1,0:T(8,128)(2,1)} %copy-done.1, f32[768,128]{1,0:T(8,128)} %get-tuple-element.30.refs_3_.refs_2_, f32[768,128]{1,0:T(8,128)} %get-tuple-element.31.refs_4_.refs_3_), custom_call_target="tpu_custom_call" | custom-call | flops 786432 | bytes 1572864 | tf_op jit(solution)/shard_map/text_rows/pallas_call | solution.py:259
  144.7 1.4 collective-permute-start.1
  146.0 2.7 %collective-permute-start.4 = (bf16[768,256]{1,0:T(8,128)(2,1)}, bf16[768,256]{1,0:T(8,128)(2,1)S(1)}, u32[]{:S(2)}, u32[]{:S(2)}) collective-permute-start(bf16[768,256]{1,0:T(8,128)(2,1)} %text_rows.5.refs_0_), channel_id=1, source_target_pairs={{0,16},{4,20},{8,24},{12,28},{16,0},{20,4},{24,8},{28,12},{1,17},{... | collective-permute-start | bytes 1179656 | tf_op jit(solution)/shard_map/text_rows/ppermute | solution.py:46
  149.0 1.8 concatenate.16.facts_ref
  151.5 1.6 collective-permute-done.29.refs_13_
  153.0 5.1 %collective-permute-done.1.refs_1_ = bf16[768,256]{1,0:T(8,128)(2,1)S(1)} collective-permute-done((bf16[768,256]{1,0:T(8,128)(2,1)}, bf16[768,256]{1,0:T(8,128)(2,1)S(1)}, u32[]{:S(2)}, u32[]{:S(2)}) %collective-permute-start.1) | collective-permute-done | bytes 393248 | tf_op jit(solution)/shard_map/text_rows/ppermute | solution.py:42
  158.2 1.6 collective-permute-start.3
  159.7 7.6 %collective-permute-done.31.refs_15_ = bf16[256,768]{1,0:T(8,128)(2,1)S(1)} collective-permute-done((bf16[256,768]{1,0:T(8,128)(2,1)S(1)}, bf16[256,768]{1,0:T(8,128)(2,1)S(1)}, u32[]{:S(2)}, u32[]{:S(2)}) %collective-permute-start.31) | collective-permute-done | bytes 393248 | tf_op jit(solution)/shard_map/visual_rows/ppermute | solution.py:46
  167.4 2.3 %collective-permute-start.5 = (bf16[768,256]{1,0:T(8,128)(2,1)S(1)}, bf16[768,256]{1,0:T(8,128)(2,1)S(1)}, u32[]{:S(2)}, u32[]{:S(2)}) collective-permute-start(bf16[768,256]{1,0:T(8,128)(2,1)S(1)} %collective-permute-done.4.refs_4_), channel_id=1, source_target_pairs={{0,4},{4,0},{8,12},{12,8},{16,20},{20,16},{24,28},{28,24},{1,5},{5... | collective-permute-start | bytes 1179656 | tf_op jit(solution)/shard_map/text_rows/ppermute | solution.py:42
  170.3 13.1 %text_rows.4.q_ref = bf16[768,512]{1,0:T(8,128)(2,1)} custom-call(s32[4]{0:T(128)} %iota.36.order_ref, s32[2]{0:T(128)} %call_exported.0.turn_ref, bf16[4,4,768,512]{3,2,1,0:T(8,128)(2,1)} %bitcast.64, bf16[8192,512]{1,0:T(8,128)(2,1)} %refs_2_.1, bf16[4,4,512]{2,1,0:T(4,128)(2,1)} %reshape.80.refs_2_.refs_4_, f32[768,128]{1,0:T(8,128)} %get-tuple-element.30.refs_3_.refs_2_, ...), custom_call_target="tpu_custom_call" | custom-call | flops 6442450944 | bytes 20971520 | tf_op jit(solution)/shard_map/text_rows/pallas_call | solution.py:217
  185.3 31.3 %attention.1 = bf16[768,512]{1,0:T(8,128)(2,1)} custom-call(s32[19]{0:T(128)} %concatenate.16.facts_ref, bf16[768,512]{1,0:T(8,128)(2,1)} %text_rows.4.q_ref, bf16[768,256]{1,0:T(8,128)(2,1)} %text_rows.5.refs_0_, bf16[768,256]{1,0:T(8,128)(2,1)} %copy-done.10, bf16[768,256]{1,0:T(8,128)(2,1)} %copy-done.13, bf16[768,256]{1,0:T(8,128)(2,1)} %copy-done.15, ...), custom_call_target="tpu_custom_call" | custom-call | flops 4718592000 | bytes 8388608 | tf_op jit(solution)/shard_map/attention/pallas_call | solution.py:379
  (99 shorter events, 16.3 us)
Async XLA Ops:
  6.5 114.9 %all-gather.3.cloned.1.call-start = ((), (), s32[]{:S(2)}) async-start(), calls=%async_computation | async-start | bytes 13369344 | tf_op jit(solution)/shard_map/text_gather/all_gather | solution.py:427
  18.5 8.6 %collective-permute-start.8 = (bf16[8,256,512]{2,1,0:T(8,128)(2,1)}, bf16[8,256,512]{2,1,0:T(8,128)(2,1)S(1)}, u32[]{:S(2)}, u32[]{:S(2)}) collective-permute-start(bf16[8,256,512]{2,1,0:T(8,128)(2,1)} %projector.3), channel_id=1, source_target_pairs={{0,32},{32,0},{64,96},{96,64},{1,33},{33,1},{65,97},{97,65},{2,34}... | collective-permute-start | bytes 6291464 | tf_op jit(solution)/shard_map/projector/ppermute | solution.py:26
  28.7 11.8 %collective-permute-start.11 = (bf16[256,512]{1,0:T(8,128)(2,1)S(1)}, bf16[256,512]{1,0:T(8,128)(2,1)S(1)}, u32[]{:S(2)}, u32[]{:S(2)}) collective-permute-start(bf16[256,512]{1,0:T(8,128)(2,1)S(1)} %get-tuple-element.18), channel_id=1, source_target_pairs={{0,64},{32,96},{64,0},{96,32},{1,65},{33,97},{65,1},{97,33},{2,66}... | collective-permute-start | bytes 786440 | tf_op jit(solution)/shard_map/projector/ppermute | solution.py:30
  29.6 12.0 %collective-permute-start.14 = (bf16[256,512]{1,0:T(8,128)(2,1)S(1)}, bf16[256,512]{1,0:T(8,128)(2,1)S(1)}, u32[]{:S(2)}, u32[]{:S(2)}) collective-permute-start(bf16[256,512]{1,0:T(8,128)(2,1)S(1)} %get-tuple-element.16), channel_id=1, source_target_pairs={{0,3},{1,0},{2,1},{3,2},{4,7},{5,4},{6,5},{7,6},{8,11},{9,8},{10,9... | collective-permute-start | bytes 786440 | tf_op jit(solution)/shard_map/projector/ppermute | solution.py:34
  33.6 10.4 %collective-permute-start.13 = (bf16[256,512]{1,0:T(8,128)(2,1)S(1)}, bf16[256,512]{1,0:T(8,128)(2,1)S(1)}, u32[]{:S(2)}, u32[]{:S(2)}) collective-permute-start(bf16[256,512]{1,0:T(8,128)(2,1)S(1)} %get-tuple-element.17), channel_id=1, source_target_pairs={{0,1},{1,2},{2,3},{3,0},{4,5},{5,6},{6,7},{7,4},{8,9},{9,10},{10,1... | collective-permute-start | bytes 786440 | tf_op jit(solution)/shard_map/projector/ppermute | solution.py:34
  33.6 16.4 %collective-permute-start.10 = (bf16[256,512]{1,0:T(8,128)(2,1)S(1)}, bf16[256,512]{1,0:T(8,128)(2,1)S(1)}, u32[]{:S(2)}, u32[]{:S(2)}) collective-permute-start(bf16[256,512]{1,0:T(8,128)(2,1)S(1)} %get-tuple-element.19), channel_id=1, source_target_pairs={{0,3},{1,0},{2,1},{3,2},{4,7},{5,4},{6,5},{7,6},{8,11},{9,8},{10,9... | collective-permute-start | bytes 786440 | tf_op jit(solution)/shard_map/projector/ppermute | solution.py:34
  36.8 14.7 %collective-permute-start.9 = (bf16[256,512]{1,0:T(8,128)(2,1)S(1)}, bf16[256,512]{1,0:T(8,128)(2,1)S(1)}, u32[]{:S(2)}, u32[]{:S(2)}) collective-permute-start(bf16[256,512]{1,0:T(8,128)(2,1)S(1)} %get-tuple-element.15), channel_id=1, source_target_pairs={{0,1},{1,2},{2,3},{3,0},{4,5},{5,6},{6,7},{7,4},{8,9},{9,10},{10,1... | collective-permute-start | bytes 786440 | tf_op jit(solution)/shard_map/projector/ppermute | solution.py:34
  45.2 10.7 %collective-permute-start.15 = (bf16[256,512]{1,0:T(8,128)(2,1)S(1)}, bf16[256,512]{1,0:T(8,128)(2,1)S(1)}, u32[]{:S(2)}, u32[]{:S(2)}) collective-permute-start(bf16[256,512]{1,0:T(8,128)(2,1)S(1)} %get-tuple-element.21), channel_id=1, source_target_pairs={{0,64},{32,96},{64,0},{96,32},{1,65},{33,97},{65,1},{97,33},{2,66}... | collective-permute-start | bytes 786440 | tf_op jit(solution)/shard_map/projector/ppermute | solution.py:30
  46.6 15.2 %collective-permute-start.12 = (bf16[256,512]{1,0:T(8,128)(2,1)S(1)}, bf16[256,512]{1,0:T(8,128)(2,1)S(1)}, u32[]{:S(2)}, u32[]{:S(2)}) collective-permute-start(bf16[256,512]{1,0:T(8,128)(2,1)S(1)} %get-tuple-element.20), channel_id=1, source_target_pairs={{0,2},{1,3},{2,0},{3,1},{4,6},{5,7},{6,4},{7,5},{8,10},{9,11},{10,... | collective-permute-start | bytes 786440 | tf_op jit(solution)/shard_map/projector/ppermute | solution.py:34
  62.9 28.8 %copy-start.18 = (s32[3]{0:T(128)S(1)}, s32[3]{0:T(128)}, u32[]{:S(2)}) copy-start(s32[3]{0:T(128)} %param.16) | copy-start | bytes 40
  62.9 29.0 %copy-start.3 = (bf16[8192]{0:T(1024)(128)(2,1)S(1)}, bf16[8192]{0:T(1024)(128)(2,1)}, u32[]{:S(2)}) copy-start(bf16[8192]{0:T(1024)(128)(2,1)} %param.12) | copy-start | bytes 49156
  63.0 31.8 %copy-start.19 = (s32[8]{0:T(128)S(1)}, s32[8]{0:T(128)}, u32[]{:S(2)}) copy-start(s32[8]{0:T(128)} %param.15) | copy-start | bytes 100
  63.0 11.1 %collective-permute-start.19 = (bf16[256,512]{1,0:T(8,128)(2,1)S(1)}, bf16[256,512]{1,0:T(8,128)(2,1)S(1)}, u32[]{:S(2)}, u32[]{:S(2)}) collective-permute-start(bf16[256,512]{1,0:T(8,128)(2,1)S(1)} %get-tuple-element.14), channel_id=1, source_target_pairs={{0,64},{32,96},{64,0},{96,32},{1,65},{33,97},{65,1},{97,33},{2,66}... | collective-permute-start | bytes 786440 | tf_op jit(solution)/shard_map/visual_gather/ppermute | solution.py:30
  64.3 13.5 %collective-permute-start.17 = (bf16[256,512]{1,0:T(8,128)(2,1)S(1)}, bf16[256,512]{1,0:T(8,128)(2,1)S(1)}, u32[]{:S(2)}, u32[]{:S(2)}) collective-permute-start(bf16[256,512]{1,0:T(8,128)(2,1)S(1)} %get-tuple-element.14), channel_id=1, source_target_pairs={{0,2},{1,3},{2,0},{3,1},{4,6},{5,7},{6,4},{7,5},{8,10},{9,11},{10,... | collective-permute-start | bytes 786440 | tf_op jit(solution)/shard_map/visual_gather/ppermute | solution.py:34
  66.1 17.9 %collective-permute-start.16 = (bf16[256,512]{1,0:T(8,128)(2,1)S(1)}, bf16[256,512]{1,0:T(8,128)(2,1)S(1)}, u32[]{:S(2)}, u32[]{:S(2)}) collective-permute-start(bf16[256,512]{1,0:T(8,128)(2,1)S(1)} %get-tuple-element.14), channel_id=1, source_target_pairs={{0,1},{1,2},{2,3},{3,0},{4,5},{5,6},{6,7},{7,4},{8,9},{9,10},{10,1... | collective-permute-start | bytes 786440 | tf_op jit(solution)/shard_map/visual_gather/ppermute | solution.py:34
  66.1 18.0 %collective-permute-start.18 = (bf16[256,512]{1,0:T(8,128)(2,1)S(1)}, bf16[256,512]{1,0:T(8,128)(2,1)S(1)}, u32[]{:S(2)}, u32[]{:S(2)}) collective-permute-start(bf16[256,512]{1,0:T(8,128)(2,1)S(1)} %get-tuple-element.14), channel_id=1, source_target_pairs={{0,3},{1,0},{2,1},{3,2},{4,7},{5,4},{6,5},{7,6},{8,11},{9,8},{10,9... | collective-permute-start | bytes 786440 | tf_op jit(solution)/shard_map/visual_gather/ppermute | solution.py:34
  74.1 17.4 %collective-permute-start.20 = (bf16[256,512]{1,0:T(8,128)(2,1)S(1)}, bf16[256,512]{1,0:T(8,128)(2,1)S(1)}, u32[]{:S(2)}, u32[]{:S(2)}) collective-permute-start(bf16[256,512]{1,0:T(8,128)(2,1)S(1)} %collective-permute-done.19), channel_id=1, source_target_pairs={{0,1},{1,2},{2,3},{3,0},{4,5},{5,6},{6,7},{7,4},{8,9},{9,10},{10,1... | collective-permute-start | bytes 786440 | tf_op jit(solution)/shard_map/visual_gather/ppermute | solution.py:34
  74.1 17.5 %collective-permute-start.22 = (bf16[256,512]{1,0:T(8,128)(2,1)S(1)}, bf16[256,512]{1,0:T(8,128)(2,1)S(1)}, u32[]{:S(2)}, u32[]{:S(2)}) collective-permute-start(bf16[256,512]{1,0:T(8,128)(2,1)S(1)} %collective-permute-done.19), channel_id=1, source_target_pairs={{0,3},{1,0},{2,1},{3,2},{4,7},{5,4},{6,5},{7,6},{8,11},{9,8},{10,9... | collective-permute-start | bytes 786440 | tf_op jit(solution)/shard_map/visual_gather/ppermute | solution.py:34
  77.7 13.8 %collective-permute-start.21 = (bf16[256,512]{1,0:T(8,128)(2,1)S(1)}, bf16[256,512]{1,0:T(8,128)(2,1)S(1)}, u32[]{:S(2)}, u32[]{:S(2)}) collective-permute-start(bf16[256,512]{1,0:T(8,128)(2,1)S(1)} %collective-permute-done.17), channel_id=1, source_target_pairs={{0,64},{32,96},{64,0},{96,32},{1,65},{33,97},{65,1},{97,33},{2,66}... | collective-permute-start | bytes 786440 | tf_op jit(solution)/shard_map/visual_gather/ppermute | solution.py:30
  91.6 7.0 %copy-start = (bf16[8,256,512]{2,1,0:T(8,128)(2,1)}, bf16[8,256,512]{2,1,0:T(8,128)(2,1)S(1)}, u32[]{:S(2)}) copy-start(bf16[8,256,512]{2,1,0:T(8,128)(2,1)S(1)} %bitcast_dynamic-update-slice_fusion) | copy-start | bytes 6291460
  91.6 7.0 %collective-permute-start.23 = (bf16[2,4,256,512]{3,2,1,0:T(8,128)(2,1)S(1)}, bf16[2,4,256,512]{3,2,1,0:T(8,128)(2,1)}, u32[]{:S(2)}, u32[]{:S(2)}) collective-permute-start(bf16[2,4,256,512]{3,2,1,0:T(8,128)(2,1)S(1)} %bitcast.65), channel_id=1, source_target_pairs={{0,32},{32,0},{64,96},{96,64},{1,33},{33,1},{65,97},{97,65},{2,34}... | collective-permute-start | bytes 6291464 | tf_op jit(solution)/shard_map/visual_gather/ppermute | solution.py:26
  108.5 6.1 %collective-permute-start.24 = (bf16[256,128]{1,0:T(8,128)(2,1)}, bf16[256,128]{1,0:T(8,128)(2,1)S(1)}, u32[]{:S(2)}, u32[]{:S(2)}) collective-permute-start(bf16[256,128]{1,0:T(8,128)(2,1)} %get-tuple-element.11.refs_0_), channel_id=1, source_target_pairs={{0,1},{1,0},{2,3},{3,2},{4,5},{5,4},{6,7},{7,6},{8,9},{9,8},{10,11... | collective-permute-start | bytes 196616 | tf_op jit(solution)/shard_map/visual_rows/ppermute | solution.py:38
  117.3 19.0 %collective-permute-start.25 = (bf16[256,768]{1,0:T(8,128)(2,1)}, bf16[256,768]{1,0:T(8,128)(2,1)S(1)}, u32[]{:S(2)}, u32[]{:S(2)}) collective-permute-start(bf16[256,768]{1,0:T(8,128)(2,1)} %visual_rows.3.refs_8_), channel_id=1, source_target_pairs={{0,4},{4,0},{8,12},{12,8},{16,20},{20,16},{24,28},{28,24},{1,5},{5... | collective-permute-start | bytes 1179656 | tf_op jit(solution)/shard_map/visual_rows/ppermute | solution.py:42
  118.6 27.4 %collective-permute-start.26 = (bf16[256,768]{1,0:T(8,128)(2,1)}, bf16[256,768]{1,0:T(8,128)(2,1)S(1)}, u32[]{:S(2)}, u32[]{:S(2)}) collective-permute-start(bf16[256,768]{1,0:T(8,128)(2,1)} %visual_rows.3.refs_8_), channel_id=1, source_target_pairs={{0,8},{4,12},{8,16},{12,20},{16,24},{20,28},{24,0},{28,4},{1,9},{5... | collective-permute-start | bytes 1179656 | tf_op jit(solution)/shard_map/visual_rows/ppermute | solution.py:46
  118.9 20.6 %collective-permute-start.28 = (bf16[256,768]{1,0:T(8,128)(2,1)}, bf16[256,768]{1,0:T(8,128)(2,1)S(1)}, u32[]{:S(2)}, u32[]{:S(2)}) collective-permute-start(bf16[256,768]{1,0:T(8,128)(2,1)} %visual_rows.3.refs_8_), channel_id=1, source_target_pairs={{0,16},{4,20},{8,24},{12,28},{16,0},{20,4},{24,8},{28,12},{1,17},{... | collective-permute-start | bytes 1179656 | tf_op jit(solution)/shard_map/visual_rows/ppermute | solution.py:46
  121.4 24.6 %collective-permute-start.30 = (bf16[256,768]{1,0:T(8,128)(2,1)}, bf16[256,768]{1,0:T(8,128)(2,1)S(1)}, u32[]{:S(2)}, u32[]{:S(2)}) collective-permute-start(bf16[256,768]{1,0:T(8,128)(2,1)} %visual_rows.3.refs_8_), channel_id=1, source_target_pairs={{0,24},{4,28},{8,0},{12,4},{16,8},{20,12},{24,16},{28,20},{1,25},{... | collective-permute-start | bytes 1179656 | tf_op jit(solution)/shard_map/visual_rows/ppermute | solution.py:46
  131.7 9.9 %collective-permute-start = (bf16[768,128]{1,0:T(8,128)(2,1)}, bf16[768,128]{1,0:T(8,128)(2,1)S(1)}, u32[]{:S(2)}, u32[]{:S(2)}) collective-permute-start(bf16[768,128]{1,0:T(8,128)(2,1)} %get-tuple-element.10.refs_0_), channel_id=1, source_target_pairs={{0,1},{1,0},{2,3},{3,2},{4,5},{5,4},{6,7},{7,6},{8,9},{9,8},{10,11... | collective-permute-start | bytes 589832 | tf_op jit(solution)/shard_map/text_rows/ppermute | solution.py:38
  136.2 47.1 %copy-start.4 = (bf16[256,768]{1,0:T(8,128)(2,1)}, bf16[256,768]{1,0:T(8,128)(2,1)S(1)}, u32[]{:S(2)}) copy-start(bf16[256,768]{1,0:T(8,128)(2,1)S(1)} %collective-permute-done.25.refs_9_) | copy-start | bytes 1179652
  136.2 14.6 %collective-permute-start.27 = (bf16[256,768]{1,0:T(8,128)(2,1)S(1)}, bf16[256,768]{1,0:T(8,128)(2,1)S(1)}, u32[]{:S(2)}, u32[]{:S(2)}) collective-permute-start(bf16[256,768]{1,0:T(8,128)(2,1)S(1)} %collective-permute-done.25.refs_9_), channel_id=1, source_target_pairs={{0,8},{4,12},{8,16},{12,20},{16,24},{20,28},{24,0},{28,4},{1,9},{5... | collective-permute-start | bytes 1179656 | tf_op jit(solution)/shard_map/visual_rows/ppermute | solution.py:46
  139.5 43.9 %copy-start.6 = (bf16[256,768]{1,0:T(8,128)(2,1)}, bf16[256,768]{1,0:T(8,128)(2,1)S(1)}, u32[]{:S(2)}) copy-start(bf16[256,768]{1,0:T(8,128)(2,1)S(1)} %collective-permute-done.28.refs_12_) | copy-start | bytes 1179652
  139.5 13.6 %collective-permute-start.29 = (bf16[256,768]{1,0:T(8,128)(2,1)S(1)}, bf16[256,768]{1,0:T(8,128)(2,1)S(1)}, u32[]{:S(2)}, u32[]{:S(2)}) collective-permute-start(bf16[256,768]{1,0:T(8,128)(2,1)S(1)} %collective-permute-done.28.refs_12_), channel_id=1, source_target_pairs={{0,4},{4,0},{8,12},{12,8},{16,20},{20,16},{24,28},{28,24},{1,5},{5... | collective-permute-start | bytes 1179656 | tf_op jit(solution)/shard_map/visual_rows/ppermute | solution.py:42
  144.7 13.5 %collective-permute-start.1 = (bf16[768,256]{1,0:T(8,128)(2,1)}, bf16[768,256]{1,0:T(8,128)(2,1)S(1)}, u32[]{:S(2)}, u32[]{:S(2)}) collective-permute-start(bf16[768,256]{1,0:T(8,128)(2,1)} %text_rows.5.refs_0_), channel_id=1, source_target_pairs={{0,4},{4,0},{8,12},{12,8},{16,20},{20,16},{24,28},{28,24},{1,5},{5... | collective-permute-start | bytes 1179656 | tf_op jit(solution)/shard_map/text_rows/ppermute | solution.py:42
  146.0 37.3 %copy-start.5 = (bf16[256,768]{1,0:T(8,128)(2,1)}, bf16[256,768]{1,0:T(8,128)(2,1)S(1)}, u32[]{:S(2)}) copy-start(bf16[256,768]{1,0:T(8,128)(2,1)S(1)} %collective-permute-done.26.refs_10_) | copy-start | bytes 1179652
  146.0 21.4 %collective-permute-start.31 = (bf16[256,768]{1,0:T(8,128)(2,1)S(1)}, bf16[256,768]{1,0:T(8,128)(2,1)S(1)}, u32[]{:S(2)}, u32[]{:S(2)}) collective-permute-start(bf16[256,768]{1,0:T(8,128)(2,1)S(1)} %collective-permute-done.25.refs_9_), channel_id=1, source_target_pairs={{0,24},{4,28},{8,0},{12,4},{16,8},{20,12},{24,16},{28,20},{1,25},{... | collective-permute-start | bytes 1179656 | tf_op jit(solution)/shard_map/visual_rows/ppermute | solution.py:46
  146.0 37.3 %copy-start.7 = (bf16[256,768]{1,0:T(8,128)(2,1)}, bf16[256,768]{1,0:T(8,128)(2,1)S(1)}, u32[]{:S(2)}) copy-start(bf16[256,768]{1,0:T(8,128)(2,1)S(1)} %collective-permute-done.30.refs_14_) | copy-start | bytes 1179652
  146.0 21.3 %collective-permute-start.4 = (bf16[768,256]{1,0:T(8,128)(2,1)}, bf16[768,256]{1,0:T(8,128)(2,1)S(1)}, u32[]{:S(2)}, u32[]{:S(2)}) collective-permute-start(bf16[768,256]{1,0:T(8,128)(2,1)} %text_rows.5.refs_0_), channel_id=1, source_target_pairs={{0,16},{4,20},{8,24},{12,28},{16,0},{20,4},{24,8},{28,12},{1,17},{... | collective-permute-start | bytes 1179656 | tf_op jit(solution)/shard_map/text_rows/ppermute | solution.py:46
  150.8 32.5 %copy-start.8 = (bf16[256,768]{1,0:T(8,128)(2,1)}, bf16[256,768]{1,0:T(8,128)(2,1)S(1)}, u32[]{:S(2)}) copy-start(bf16[256,768]{1,0:T(8,128)(2,1)S(1)} %collective-permute-done.27.refs_11_) | copy-start | bytes 1179652
  150.8 32.6 %collective-permute-start.2 = (bf16[768,256]{1,0:T(8,128)(2,1)}, bf16[768,256]{1,0:T(8,128)(2,1)S(1)}, u32[]{:S(2)}, u32[]{:S(2)}) collective-permute-start(bf16[768,256]{1,0:T(8,128)(2,1)} %text_rows.5.refs_0_), channel_id=1, source_target_pairs={{0,8},{4,12},{8,16},{12,20},{16,24},{20,28},{24,0},{28,4},{1,9},{5... | collective-permute-start | bytes 1179656 | tf_op jit(solution)/shard_map/text_rows/ppermute | solution.py:46
  153.0 30.3 %copy-start.9 = (bf16[256,768]{1,0:T(8,128)(2,1)}, bf16[256,768]{1,0:T(8,128)(2,1)S(1)}, u32[]{:S(2)}) copy-start(bf16[256,768]{1,0:T(8,128)(2,1)S(1)} %collective-permute-done.29.refs_13_) | copy-start | bytes 1179652
  153.0 30.4 %collective-permute-start.6 = (bf16[768,256]{1,0:T(8,128)(2,1)}, bf16[768,256]{1,0:T(8,128)(2,1)S(1)}, u32[]{:S(2)}, u32[]{:S(2)}) collective-permute-start(bf16[768,256]{1,0:T(8,128)(2,1)} %text_rows.5.refs_0_), channel_id=1, source_target_pairs={{0,24},{4,28},{8,0},{12,4},{16,8},{20,12},{24,16},{28,20},{1,25},{... | collective-permute-start | bytes 1179656 | tf_op jit(solution)/shard_map/text_rows/ppermute | solution.py:46
  158.2 25.2 %copy-start.10 = (bf16[768,256]{1,0:T(8,128)(2,1)}, bf16[768,256]{1,0:T(8,128)(2,1)S(1)}, u32[]{:S(2)}) copy-start(bf16[768,256]{1,0:T(8,128)(2,1)S(1)} %collective-permute-done.1.refs_1_) | copy-start | bytes 1179652
  158.2 25.3 %collective-permute-start.3 = (bf16[768,256]{1,0:T(8,128)(2,1)S(1)}, bf16[768,256]{1,0:T(8,128)(2,1)S(1)}, u32[]{:S(2)}, u32[]{:S(2)}) collective-permute-start(bf16[768,256]{1,0:T(8,128)(2,1)S(1)} %collective-permute-done.1.refs_1_), channel_id=1, source_target_pairs={{0,8},{4,12},{8,16},{12,20},{16,24},{20,28},{24,0},{28,4},{1,9},{5... | collective-permute-start | bytes 1179656 | tf_op jit(solution)/shard_map/text_rows/ppermute | solution.py:46
  167.4 16.0 %copy-start.11 = (bf16[256,768]{1,0:T(8,128)(2,1)}, bf16[256,768]{1,0:T(8,128)(2,1)S(1)}, u32[]{:S(2)}) copy-start(bf16[256,768]{1,0:T(8,128)(2,1)S(1)} %collective-permute-done.31.refs_15_) | copy-start | bytes 1179652
  167.4 16.1 %collective-permute-start.7 = (bf16[768,256]{1,0:T(8,128)(2,1)S(1)}, bf16[768,256]{1,0:T(8,128)(2,1)S(1)}, u32[]{:S(2)}, u32[]{:S(2)}) collective-permute-start(bf16[768,256]{1,0:T(8,128)(2,1)S(1)} %collective-permute-done.1.refs_1_), channel_id=1, source_target_pairs={{0,24},{4,28},{8,0},{12,4},{16,8},{20,12},{24,16},{28,20},{1,25},{... | collective-permute-start | bytes 1179656 | tf_op jit(solution)/shard_map/text_rows/ppermute | solution.py:46
  167.4 16.0 %copy-start.12 = (bf16[768,256]{1,0:T(8,128)(2,1)}, bf16[768,256]{1,0:T(8,128)(2,1)S(1)}, u32[]{:S(2)}) copy-start(bf16[768,256]{1,0:T(8,128)(2,1)S(1)} %collective-permute-done.4.refs_4_) | copy-start | bytes 1179652
  167.4 16.1 %collective-permute-start.5 = (bf16[768,256]{1,0:T(8,128)(2,1)S(1)}, bf16[768,256]{1,0:T(8,128)(2,1)S(1)}, u32[]{:S(2)}, u32[]{:S(2)}) collective-permute-start(bf16[768,256]{1,0:T(8,128)(2,1)S(1)} %collective-permute-done.4.refs_4_), channel_id=1, source_target_pairs={{0,4},{4,0},{8,12},{12,8},{16,20},{20,16},{24,28},{28,24},{1,5},{5... | collective-permute-start | bytes 1179656 | tf_op jit(solution)/shard_map/text_rows/ppermute | solution.py:42
  183.5 1.0 copy-start.15
  183.5 1.1 copy-start.17
  (5 other events, 3.7 us)
Sparse Core Ops, SparseCore 0:
  9.0 109.9 all-gather.2
